TPU v7x, 256 devices: a whole 4x4x8 slice. The times are simulated.
256 devices in a mesh: seq: 32 (over y, z), head: 2 (over core), pool: 4 (over x).
Axes of the slice: x: 4, y: 4, z: 8, core: 2. Of those that a mesh axis runs over, the one named last changes fastest.
Arguments:
- prefill_hidden: bfloat16 [4096, 7168], P('seq', ('head', 'pool')), may hold values from -6 to 6
- down_weight: bfloat16 [7168, 576], P(('head', 'pool')), may hold values from -0.0625 to 0.0625
- latent_gain: float32 [512], replicated, may hold values from 0.1 to 1.9
- key_weight: bfloat16 [512, 16384], P(None, ('head', 'pool')), may hold values from -0.25 to 0.25
- value_weight: bfloat16 [512, 16384], P(None, ('head', 'pool')), may hold values from -0.25 to 0.25
- prefill_query: bfloat16 [4096, 24576], P('seq', ('head', 'pool')), may hold values from -240 to 240
- decode_hidden: bfloat16 [2, 128, 7168], P(None, 'seq', ('head', 'pool')), may hold values from -6 to 6
- decode_query: bfloat16 [2, 128, 24576], P(None, 'seq', ('head', 'pool')), may hold values from -240 to 240
- latent_cache: bfloat16 [128, 512, 576], P('seq'), may hold values from -6 to 6
- place_device: int32 [4096], P('seq'), may hold values from 0 to 31, as said below
- place_slot: int32 [4096], P('seq'), may hold values from 0 to 2047, as said below
- context_length: int32 [128], P('seq'), may hold values from 1 to 512, as said below
Outputs:
- prefill_out: bfloat16 [4096, 16384], P('seq', ('head', 'pool'))
- decode_out: bfloat16 [2, 128, 16384], P(None, 'seq', ('head', 'pool'))
Inputs may be any that keep to these rules, and one draw needn't show every extreme that they name: `place_device`: each block of 128 consecutive tokens sends at most 8 tokens to one decode index, and exactly 8 to one of them. With place_device every token names its own slot; the position place_slot % 512 is below context_length of the row it names. `context_length`: some row has exactly 512.
All inputs are finite; a program needn't handle non-finite values.
Results may differ from a plain program's by a relative error of at most 0.012.
The roundings to bfloat16 on the way count: a program that leaves them out, or rounds other values in their place, can miss the bound.
Values may be sent and summed in bfloat16 or wider, within the bound.
A program may use at most 64 MiB of HBM per device.

v0:
```python
import math

import jax
import jax.numpy as jnp
from jax import lax
from jax.sharding import PartitionSpec as P

LAT = 512
ROPE = 64
NOPE = 128
VDIM = 128
PROMPTS = 1


def rotate(part, position):
    half = part.shape[-1] // 2
    freq = 10000.0 ** (-jnp.arange(half, dtype=jnp.float32) / half)
    angle = position[..., None] * freq
    first_half = part[..., :half]
    second_half = part[..., half:]
    cosine = jnp.cos(angle)
    sine = jnp.sin(angle)
    return jnp.concatenate(
        [first_half * cosine - second_half * sine, second_half * cosine + first_half * sine], -1
    )


def finalize(summed, latent_gain, position):
    content = summed[..., :LAT]
    meansq = jnp.mean(content * content, -1, keepdims=True)
    content = content * lax.rsqrt(meansq + 1e-06) * latent_gain
    return jnp.concatenate([content, rotate(summed[..., LAT:], position)], -1).astype(jnp.bfloat16)


def on_device(
    prefill_hidden,
    down_weight,
    latent_gain,
    key_weight,
    value_weight,
    prefill_query,
    decode_hidden,
    decode_query,
    latent_cache,
    place_device,
    place_slot,
    context_length,
):
    tok_rows = prefill_hidden.shape[0]
    seq_count = lax.axis_size("seq")
    seq_index = lax.axis_index("seq")
    group = seq_count // PROMPTS
    prompt_len = tok_rows * group
    row_width = LAT + ROPE
    heads = prefill_query.shape[1] // (NOPE + ROPE)
    factor = (NOPE + ROPE) ** (-0.5)
    prefill_part = jnp.dot(prefill_hidden, down_weight, preferred_element_type=jnp.float32)
    decode_part = jnp.einsum(
        "srd,dc->src", decode_hidden, down_weight, preferred_element_type=jnp.float32
    )
    prefill_sum, decode_sum = lax.psum((prefill_part, decode_part), ("head", "pool"))
    first = seq_index * tok_rows
    token_index = first + jnp.arange(tok_rows, dtype=jnp.int32)
    latent = finalize(prefill_sum, latent_gain, (token_index % prompt_len).astype(jnp.float32))
    prompt_first = first // prompt_len * prompt_len
    query = prefill_query.reshape(tok_rows, heads, NOPE + ROPE)
    query_nope = query[:, :, :NOPE]
    query_rope = query[:, :, NOPE:]

    def attend_block(carry, block, key_start):
        running, total, accumulated = carry
        count = block.shape[0]
        content = block[:, :LAT]
        knope = (
            jnp.dot(content, key_weight, preferred_element_type=jnp.float32)
            .astype(jnp.bfloat16)
            .reshape(count, heads, NOPE)
        )
        values = (
            jnp.dot(content, value_weight, preferred_element_type=jnp.float32)
            .astype(jnp.bfloat16)
            .reshape(count, heads, VDIM)
        )
        scores = jnp.einsum("qhd,khd->qhk", query_nope, knope, preferred_element_type=jnp.float32)
        scores = scores + jnp.einsum(
            "qhd,kd->qhk", query_rope, block[:, LAT:], preferred_element_type=jnp.float32
        )
        key_index = key_start + jnp.arange(count, dtype=jnp.int32)
        allowed = (key_index[None, :] <= token_index[:, None]) & (
            key_index[None, :] >= prompt_first
        )
        allowed = allowed[:, None, :]
        scores = jnp.where(allowed, scores * factor, -1e30)
        peak = jnp.maximum(running, jnp.max(scores, -1))
        shrink = jnp.exp(running - peak)
        expo = jnp.where(allowed, jnp.exp(scores - peak[..., None]), 0.0)
        total = total * shrink + jnp.sum(expo, -1)
        accumulated = accumulated * shrink[..., None] + jnp.einsum(
            "qhk,khd->qhd", expo.astype(jnp.bfloat16), values, preferred_element_type=jnp.float32
        )
        return (peak, total, accumulated)

    def guarded(carry, block, key_start):
        count = block.shape[0]
        needed = (key_start <= first + tok_rows - 1) & (key_start + count - 1 >= prompt_first)
        return lax.cond(
            needed, lambda state: attend_block(state, block, key_start), lambda state: state, carry
        )

    initial = (
        jnp.full((tok_rows, heads), -1e30, jnp.float32),
        jnp.zeros((tok_rows, heads), jnp.float32),
        jnp.zeros((tok_rows, heads, VDIM), jnp.float32),
    )
    carry = initial
    block = lax.all_gather(latent, "seq", axis=0, tiled=True)
    count = block.shape[0]
    span = math.gcd(count, 512)
    pieces = block.reshape(count // span, span, block.shape[1])
    starts = span * jnp.arange(count // span, dtype=jnp.int32)

    def advance(state, item):
        return (guarded(state, item[0], item[1]), None)

    carry, unused = lax.scan(advance, carry, (pieces, starts))
    running, total, accumulated = carry
    prefill_out = (
        (accumulated / total[..., None]).astype(jnp.bfloat16).reshape(tok_rows, heads * VDIM)
    )
    rows = latent_cache.shape[0]
    slots_per_row = latent_cache.shape[1]
    flat_cache = latent_cache.reshape(rows * slots_per_row, row_width)
    capacity = 2 * -(-tok_rows // seq_count)
    marks = (place_device[:, None] == jnp.arange(seq_count, dtype=jnp.int32)[None, :]).astype(
        jnp.int32
    )
    arrival = jnp.sum((jnp.cumsum(marks, 0) - marks) * marks, 1)
    position = place_device * capacity + arrival
    outgoing = (
        jnp.zeros((seq_count * capacity, row_width), jnp.bfloat16)
        .at[position]
        .set(latent, mode="drop")
    )
    out_slots = (
        jnp.full((seq_count * capacity,), rows * slots_per_row, jnp.int32)
        .at[position]
        .set(place_slot, mode="drop")
    )
    incoming, in_slots = (
        lax.all_to_all(
            outgoing.reshape(seq_count, capacity, row_width),
            "seq",
            split_axis=0,
            concat_axis=0,
            tiled=True,
        ),
        lax.all_to_all(
            out_slots.reshape(seq_count, capacity), "seq", split_axis=0, concat_axis=0, tiled=True
        ),
    )
    flat_cache = flat_cache.at[in_slots.reshape(-1)].set(
        incoming.reshape(-1, row_width), mode="drop"
    )
    filled = flat_cache.reshape(rows, slots_per_row, row_width)
    steps = decode_hidden.shape[0]
    new_position = (context_length[None, :] + jnp.arange(steps, dtype=jnp.int32)[:, None]).astype(
        jnp.float32
    )
    fresh = finalize(decode_sum, latent_gain, new_position)
    step_query = decode_query.reshape(steps, rows, heads, NOPE + ROPE)
    absorbed = jnp.einsum(
        "srhd,chd->srhc",
        step_query[..., :NOPE],
        key_weight.reshape(LAT, heads, NOPE),
        preferred_element_type=jnp.float32,
    ).astype(jnp.bfloat16)
    full_query = jnp.concatenate([absorbed, step_query[..., NOPE:]], -1)
    valid = (jnp.arange(slots_per_row, dtype=jnp.int32)[None, :] < context_length[:, None])[
        :, None, :
    ]
    value_rows = value_weight.reshape(LAT, heads, VDIM)
    results = []
    for step in range(steps):
        current = full_query[step]
        recent = fresh[: step + 1]
        older = jnp.einsum("rhc,rkc->rhk", current, filled, preferred_element_type=jnp.float32)
        older = jnp.where(valid, older * factor, -1e30)
        newer = (
            jnp.einsum("rhc,trc->rht", current, recent, preferred_element_type=jnp.float32) * factor
        )
        peak = jnp.maximum(jnp.max(older, -1), jnp.max(newer, -1))[..., None]
        older_exp = jnp.where(valid, jnp.exp(older - peak), 0.0)
        newer_exp = jnp.exp(newer - peak)
        total_weight = jnp.sum(older_exp, -1) + jnp.sum(newer_exp, -1)
        mixed = jnp.einsum(
            "rhk,rkc->rhc",
            older_exp.astype(jnp.bfloat16),
            filled[..., :LAT],
            preferred_element_type=jnp.float32,
        )
        mixed = mixed + jnp.einsum(
            "rht,trc->rhc",
            newer_exp.astype(jnp.bfloat16),
            recent[..., :LAT],
            preferred_element_type=jnp.float32,
        )
        mixed = (mixed / total_weight[..., None]).astype(jnp.bfloat16)
        output = jnp.einsum(
            "rhc,chd->rhd", mixed, value_rows, preferred_element_type=jnp.float32
        ).astype(jnp.bfloat16)
        results.append(output.reshape(rows, heads * VDIM))
    decode_out = jnp.stack(results)
    return (prefill_out, decode_out)


def solution(mesh):
    in_specs = (
        P("seq", ("head", "pool")),
        P(("head", "pool"), None),
        P(),
        P(None, ("head", "pool")),
        P(None, ("head", "pool")),
        P("seq", ("head", "pool")),
        P(None, "seq", ("head", "pool")),
        P(None, "seq", ("head", "pool")),
        P("seq", None, None),
        P("seq"),
        P("seq"),
        P("seq"),
    )
    out_specs = (P("seq", ("head", "pool")), P(None, "seq", ("head", "pool")))
    return jax.shard_map(
        on_device, mesh=mesh, in_specs=in_specs, out_specs=out_specs, check_vma=False
    )
```

profile of v0, /device:TPU:252, one launch (start us, length us, event | category | flops | bytes accessed | tf_op | source)
XLA Modules:
  0.0 369.2 jit_solution(11567905708583399920)
XLA Ops:
  10.6 60.6 %all-reduce.2.cloned.1.call-done = f32[128,576]{0,1:T(8,128)} async-done(((f32[128,576]{0,1:T(8,128)}), f32[128,576]{0,1:T(8,128)}) %all-reduce.2.cloned.1.call-update) | async-done | bytes 294928 | tf_op jit(solution)/shard_map/psum | solution.py:61
  77.1 9.6 %all-to-all-start = ((s32[32,1,8]{2,1,0:T(1,128)}), s32[32,1,8]{2,1,0:T(1,128)S(1)}, u32[]{:S(2)}, u32[]{:S(2)}) async-start(s32[32,1,8]{2,1,0:T(1,128)} %bitcast.12), calls=%async_computation | async-start | bytes 32768 | tf_op jit(solution)/shard_map/all_to_all | solution.py:157
  89.5 27.5 %psum.15 = f32[2,4,576]{2,1,0:T(4,128)S(1)} all-reduce(f32[2,4,576]{2,1,0:T(4,128)S(1)} %fusion.67), channel_id=1, replica_groups=mesh['seq'=32,'head'=2,'pool'=4] {'head','pool'}, use_global_device_ids=true, to_apply=%region_14.15 | all-reduce | flops 4608 | bytes 36864 | tf_op jit(solution)/shard_map/psum | solution.py:61
  120.5 9.8 %all-to-all-start.1 = ((bf16[32,8,576]{2,1,0:T(8,128)(2,1)}), bf16[32,8,576]{2,1,0:T(8,128)(2,1)S(1)}, u32[]{:S(2)}, u32[]{:S(2)}) async-start(bf16[32,8,576]{2,1,0:T(8,128)(2,1)} %bitcast.14), calls=%async_computation.1 | async-start | bytes 655360 | tf_op jit(solution)/shard_map/all_to_all | solution.py:150
  132.0 4.3 %copy.114 = bf16[4,512,576]{2,1,0:T(8,128)(2,1)} copy(bf16[4,512,576]{1,2,0:T(8,128)(2,1)} %param.24) | data formatting | bytes 4718592 | tf_op jit(solution)/shard_map/reshape | solution.py:132
  138.8 4.3 %all-to-all-done.1 = bf16[32,8,576]{2,1,0:T(8,128)(2,1)S(1)} async-done(((bf16[32,8,576]{2,1,0:T(8,128)(2,1)}), bf16[32,8,576]{2,1,0:T(8,128)(2,1)S(1)}, u32[]{:S(2)}, u32[]{:S(2)}) %all-to-all-start.1) | async-done | bytes 294944 | tf_op jit(solution)/shard_map/all_to_all | solution.py:150
  143.1 5.3 %scatter_custom_fusion.2 = bf16[2048,576]{1,0:T(8,128)(2,1)} fusion(bf16[2048,576]{1,0:T(8,128)(2,1)} %bitcast.104, s32[256]{0:T(256)S(1)} %bitcast.117, bf16[32,8,576]{2,1,0:T(8,128)(2,1)S(1)} %all-to-all-done.1), kind=kCustom, calls=%fused_computation.66 | custom fusion | bytes 2686976 | tf_op jit(solution)/shard_map/scatter | solution.py:161
  148.4 2.8 fusion.129
  155.6 15.9 %all-gather.2.cloned.1.call-done = bf16[4096,576]{0,1:T(8,128)(2,1)} async-done(((bf16[128,576]{0,1:T(8,128)(2,1)}), bf16[4096,576]{0,1:T(8,128)(2,1)}) %all-gather.2.cloned.1.call-update) | async-done | bytes 4718608 | tf_op jit(solution)/shard_map/all_gather | solution.py:116
  171.4 4.9 %copy.180 = bf16[72,8,8,512]{3,2,0,1:T(8,128)(2,1)} copy(bf16[72,8,8,512]{3,2,1,0:T(8,128)(2,1)} %bitcast.110) | data formatting | bytes 9437184 | tf_op jit(solution)/shard_map/reshape | solution.py:119
  177.4 182.6 %while.20 = (s32[]{:T(128)}, f32[128,16]{0,1:T(8,128)S(1)}, f32[128,16]{0,1:T(8,128)S(1)}, f32[128,16,128]{0,2,1:T(8,128)}, s32[8]{0:T(128)S(1)}, /*index=5*/s32...) while((s32[]{:T(128)}, f32[128,16]{0,1:T(8,128)S(1)}, ...), condition=%wide.region_7.8_spmd.clone, body=%wide.region_2.7_spmd.clone.sunk | while | flops 2831816192 | bytes 68492720 | solution.py:125
  179.2 21.1 %conditional.3 = ((f32[128,16]{0,1:T(8,128)S(1)}, f32[128,16]{0,1:T(8,128)S(1)}, f32[128,16,128]{0,2,1:T(8,128)})) conditional(s32[]{:T(128)} %convert_element_type.133, (f32[128,16]{0,1:T(8,128)S(1)}, f32[128,16]{0,1:T(8,128)S(1)}, f32[128,16,128]{0,2,1:T(8,128)}) %tuple.78, (s32[]{:T(128)}, s32[]{:T(128)}, s32[]{:T(128)}, ...), branch_computations={%region_3.3_spmd, %region_4.6_spmd} | conditional | flops 2831816192 | bytes 68491888 | solution.py:106
  181.6 2.9 fusion.14
  190.4 2.7 convolution_convert_fusion
  193.0 2.9 copy.110
  195.9 4.4 %fusion.18 = f32[128,16,128]{0,2,1:T(8,128)} fusion(bf16[512,16,128]{0,2,1:T(8,128)(2,1)S(1)} %bitcast.103, f32[128,16,512]{0,2,1:T(8,128)} %copy-done.1, f32[128,16]{0,1:T(8,128)S(1)} %max.13, pred[128,512]{0,1:T(8,128)(4,1)S(1)} %compare_and_fusion, f32[128,16,128]{0,2,1:T(8,128)} %get-tuple-element.364, f32[128,16]{0,1:T(8,128)S(1)} %get-tuple-element.505), kind=kOutput, calls=%fused_computation.21 | convolution fusion | flops 272105472 | bytes 8470528 | tf_op jit(solution)/shard_map/while/body/eval_jaxpr/cond/branch_1_fun/qhk,khd->qhd/dot_general | solution.py:98
  202.0 21.1 %conditional.3 = ((f32[128,16]{0,1:T(8,128)S(1)}, f32[128,16]{0,1:T(8,128)S(1)}, f32[128,16,128]{0,2,1:T(8,128)})) conditional(s32[]{:T(128)} %convert_element_type.133, (f32[128,16]{0,1:T(8,128)S(1)}, f32[128,16]{0,1:T(8,128)S(1)}, f32[128,16,128]{0,2,1:T(8,128)}) %tuple.78, (s32[]{:T(128)}, s32[]{:T(128)}, s32[]{:T(128)}, ...), branch_computations={%region_3.3_spmd, %region_4.6_spmd} | conditional | flops 2831816192 | bytes 68491888 | solution.py:106
  204.5 2.9 fusion.14
  213.2 2.7 convolution_convert_fusion
  215.8 2.9 copy.110
  218.7 4.4 %fusion.18 = f32[128,16,128]{0,2,1:T(8,128)} fusion(bf16[512,16,128]{0,2,1:T(8,128)(2,1)S(1)} %bitcast.103, f32[128,16,512]{0,2,1:T(8,128)} %copy-done.1, f32[128,16]{0,1:T(8,128)S(1)} %max.13, pred[128,512]{0,1:T(8,128)(4,1)S(1)} %compare_and_fusion, f32[128,16,128]{0,2,1:T(8,128)} %get-tuple-element.364, f32[128,16]{0,1:T(8,128)S(1)} %get-tuple-element.505), kind=kOutput, calls=%fused_computation.21 | convolution fusion | flops 272105472 | bytes 8470528 | tf_op jit(solution)/shard_map/while/body/eval_jaxpr/cond/branch_1_fun/qhk,khd->qhd/dot_general | solution.py:98
  224.8 21.1 %conditional.3 = ((f32[128,16]{0,1:T(8,128)S(1)}, f32[128,16]{0,1:T(8,128)S(1)}, f32[128,16,128]{0,2,1:T(8,128)})) conditional(s32[]{:T(128)} %convert_element_type.133, (f32[128,16]{0,1:T(8,128)S(1)}, f32[128,16]{0,1:T(8,128)S(1)}, f32[128,16,128]{0,2,1:T(8,128)}) %tuple.78, (s32[]{:T(128)}, s32[]{:T(128)}, s32[]{:T(128)}, ...), branch_computations={%region_3.3_spmd, %region_4.6_spmd} | conditional | flops 2831816192 | bytes 68491888 | solution.py:106
  227.3 2.9 fusion.14
  236.0 2.7 convolution_convert_fusion
  238.7 2.9 copy.110
  241.5 4.4 %fusion.18 = f32[128,16,128]{0,2,1:T(8,128)} fusion(bf16[512,16,128]{0,2,1:T(8,128)(2,1)S(1)} %bitcast.103, f32[128,16,512]{0,2,1:T(8,128)} %copy-done.1, f32[128,16]{0,1:T(8,128)S(1)} %max.13, pred[128,512]{0,1:T(8,128)(4,1)S(1)} %compare_and_fusion, f32[128,16,128]{0,2,1:T(8,128)} %get-tuple-element.364, f32[128,16]{0,1:T(8,128)S(1)} %get-tuple-element.505), kind=kOutput, calls=%fused_computation.21 | convolution fusion | flops 272105472 | bytes 8470528 | tf_op jit(solution)/shard_map/while/body/eval_jaxpr/cond/branch_1_fun/qhk,khd->qhd/dot_general | solution.py:98
  247.6 21.1 %conditional.3 = ((f32[128,16]{0,1:T(8,128)S(1)}, f32[128,16]{0,1:T(8,128)S(1)}, f32[128,16,128]{0,2,1:T(8,128)})) conditional(s32[]{:T(128)} %convert_element_type.133, (f32[128,16]{0,1:T(8,128)S(1)}, f32[128,16]{0,1:T(8,128)S(1)}, f32[128,16,128]{0,2,1:T(8,128)}) %tuple.78, (s32[]{:T(128)}, s32[]{:T(128)}, s32[]{:T(128)}, ...), branch_computations={%region_3.3_spmd, %region_4.6_spmd} | conditional | flops 2831816192 | bytes 68491888 | solution.py:106
  250.1 2.9 fusion.14
  258.8 2.7 convolution_convert_fusion
  261.5 2.9 copy.110
  264.3 4.4 %fusion.18 = f32[128,16,128]{0,2,1:T(8,128)} fusion(bf16[512,16,128]{0,2,1:T(8,128)(2,1)S(1)} %bitcast.103, f32[128,16,512]{0,2,1:T(8,128)} %copy-done.1, f32[128,16]{0,1:T(8,128)S(1)} %max.13, pred[128,512]{0,1:T(8,128)(4,1)S(1)} %compare_and_fusion, f32[128,16,128]{0,2,1:T(8,128)} %get-tuple-element.364, f32[128,16]{0,1:T(8,128)S(1)} %get-tuple-element.505), kind=kOutput, calls=%fused_computation.21 | convolution fusion | flops 272105472 | bytes 8470528 | tf_op jit(solution)/shard_map/while/body/eval_jaxpr/cond/branch_1_fun/qhk,khd->qhd/dot_general | solution.py:98
  270.4 21.1 %conditional.3 = ((f32[128,16]{0,1:T(8,128)S(1)}, f32[128,16]{0,1:T(8,128)S(1)}, f32[128,16,128]{0,2,1:T(8,128)})) conditional(s32[]{:T(128)} %convert_element_type.133, (f32[128,16]{0,1:T(8,128)S(1)}, f32[128,16]{0,1:T(8,128)S(1)}, f32[128,16,128]{0,2,1:T(8,128)}) %tuple.78, (s32[]{:T(128)}, s32[]{:T(128)}, s32[]{:T(128)}, ...), branch_computations={%region_3.3_spmd, %region_4.6_spmd} | conditional | flops 2831816192 | bytes 68491888 | solution.py:106
  272.9 2.9 fusion.14
  281.6 2.7 convolution_convert_fusion
  284.3 2.9 copy.110
  287.2 4.4 %fusion.18 = f32[128,16,128]{0,2,1:T(8,128)} fusion(bf16[512,16,128]{0,2,1:T(8,128)(2,1)S(1)} %bitcast.103, f32[128,16,512]{0,2,1:T(8,128)} %copy-done.1, f32[128,16]{0,1:T(8,128)S(1)} %max.13, pred[128,512]{0,1:T(8,128)(4,1)S(1)} %compare_and_fusion, f32[128,16,128]{0,2,1:T(8,128)} %get-tuple-element.364, f32[128,16]{0,1:T(8,128)S(1)} %get-tuple-element.505), kind=kOutput, calls=%fused_computation.21 | convolution fusion | flops 272105472 | bytes 8470528 | tf_op jit(solution)/shard_map/while/body/eval_jaxpr/cond/branch_1_fun/qhk,khd->qhd/dot_general | solution.py:98
  293.3 21.1 %conditional.3 = ((f32[128,16]{0,1:T(8,128)S(1)}, f32[128,16]{0,1:T(8,128)S(1)}, f32[128,16,128]{0,2,1:T(8,128)})) conditional(s32[]{:T(128)} %convert_element_type.133, (f32[128,16]{0,1:T(8,128)S(1)}, f32[128,16]{0,1:T(8,128)S(1)}, f32[128,16,128]{0,2,1:T(8,128)}) %tuple.78, (s32[]{:T(128)}, s32[]{:T(128)}, s32[]{:T(128)}, ...), branch_computations={%region_3.3_spmd, %region_4.6_spmd} | conditional | flops 2831816192 | bytes 68491888 | solution.py:106
  295.7 2.9 fusion.14
  307.1 2.9 copy.110
  310.0 4.4 %fusion.18 = f32[128,16,128]{0,2,1:T(8,128)} fusion(bf16[512,16,128]{0,2,1:T(8,128)(2,1)S(1)} %bitcast.103, f32[128,16,512]{0,2,1:T(8,128)} %copy-done.1, f32[128,16]{0,1:T(8,128)S(1)} %max.13, pred[128,512]{0,1:T(8,128)(4,1)S(1)} %compare_and_fusion, f32[128,16,128]{0,2,1:T(8,128)} %get-tuple-element.364, f32[128,16]{0,1:T(8,128)S(1)} %get-tuple-element.505), kind=kOutput, calls=%fused_computation.21 | convolution fusion | flops 272105472 | bytes 8470528 | tf_op jit(solution)/shard_map/while/body/eval_jaxpr/cond/branch_1_fun/qhk,khd->qhd/dot_general | solution.py:98
  316.1 21.1 %conditional.3 = ((f32[128,16]{0,1:T(8,128)S(1)}, f32[128,16]{0,1:T(8,128)S(1)}, f32[128,16,128]{0,2,1:T(8,128)})) conditional(s32[]{:T(128)} %convert_element_type.133, (f32[128,16]{0,1:T(8,128)S(1)}, f32[128,16]{0,1:T(8,128)S(1)}, f32[128,16,128]{0,2,1:T(8,128)}) %tuple.78, (s32[]{:T(128)}, s32[]{:T(128)}, s32[]{:T(128)}, ...), branch_computations={%region_3.3_spmd, %region_4.6_spmd} | conditional | flops 2831816192 | bytes 68491888 | solution.py:106
  318.6 2.9 fusion.14
  329.9 2.9 copy.110
  332.8 4.4 %fusion.18 = f32[128,16,128]{0,2,1:T(8,128)} fusion(bf16[512,16,128]{0,2,1:T(8,128)(2,1)S(1)} %bitcast.103, f32[128,16,512]{0,2,1:T(8,128)} %copy-done.1, f32[128,16]{0,1:T(8,128)S(1)} %max.13, pred[128,512]{0,1:T(8,128)(4,1)S(1)} %compare_and_fusion, f32[128,16,128]{0,2,1:T(8,128)} %get-tuple-element.364, f32[128,16]{0,1:T(8,128)S(1)} %get-tuple-element.505), kind=kOutput, calls=%fused_computation.21 | convolution fusion | flops 272105472 | bytes 8470528 | tf_op jit(solution)/shard_map/while/body/eval_jaxpr/cond/branch_1_fun/qhk,khd->qhd/dot_general | solution.py:98
  338.9 21.1 %conditional.3 = ((f32[128,16]{0,1:T(8,128)S(1)}, f32[128,16]{0,1:T(8,128)S(1)}, f32[128,16,128]{0,2,1:T(8,128)})) conditional(s32[]{:T(128)} %convert_element_type.133, (f32[128,16]{0,1:T(8,128)S(1)}, f32[128,16]{0,1:T(8,128)S(1)}, f32[128,16,128]{0,2,1:T(8,128)}) %tuple.78, (s32[]{:T(128)}, s32[]{:T(128)}, s32[]{:T(128)}, ...), branch_computations={%region_3.3_spmd, %region_4.6_spmd} | conditional | flops 2831816192 | bytes 68491888 | solution.py:106
  341.4 2.9 fusion.14
  352.8 2.9 copy.110
  355.6 4.4 %fusion.18 = f32[128,16,128]{0,2,1:T(8,128)} fusion(bf16[512,16,128]{0,2,1:T(8,128)(2,1)S(1)} %bitcast.103, f32[128,16,512]{0,2,1:T(8,128)} %copy-done.1, f32[128,16]{0,1:T(8,128)S(1)} %max.13, pred[128,512]{0,1:T(8,128)(4,1)S(1)} %compare_and_fusion, f32[128,16,128]{0,2,1:T(8,128)} %get-tuple-element.364, f32[128,16]{0,1:T(8,128)S(1)} %get-tuple-element.505), kind=kOutput, calls=%fused_computation.21 | convolution fusion | flops 272105472 | bytes 8470528 | tf_op jit(solution)/shard_map/while/body/eval_jaxpr/cond/branch_1_fun/qhk,khd->qhd/dot_general | solution.py:98
  (224 shorter events, 105.8 us)
Async XLA Ops:
  7.2 1.2 copy-start
  7.2 67.7 %copy-start.7 = (s32[128]{0:T(128)S(1)}, s32[128]{0:T(128)}, u32[]{:S(2)}) copy-start(s32[128]{0:T(128)} %param.25) | copy-start | bytes 1540
  7.2 79.5 %copy-start.4 = (bf16[2,4,3072]{2,1,0:T(4,128)(2,1)S(1)}, bf16[2,4,3072]{2,1,0:T(4,128)(2,1)}, u32[]{:S(2)}) copy-start(bf16[2,4,3072]{2,1,0:T(4,128)(2,1)} %param.23) | copy-start | bytes 147460
  7.2 64.0 %all-reduce.2.cloned.1.call-start = ((), (), s32[]{:S(2)}) async-start(), calls=%async_computation.2 | async-start | bytes 589824 | tf_op jit(solution)/shard_map/psum | solution.py:61
  10.5 160.9 %all-gather.2.cloned.1.call-start = ((), (), s32[]{:S(2)}) async-start(), calls=%async_computation.3 | async-start | bytes 4866048 | tf_op jit(solution)/shard_map/all_gather | solution.py:116
  74.2 15.0 %copy-start.5 = (bf16[2,4,896]{2,1,0:T(4,128)(2,1)S(1)}, bf16[2,4,896]{2,1,0:T(4,128)(2,1)}, u32[]{:S(2)}) copy-start(bf16[2,4,896]{2,1,0:T(4,128)(2,1)} %param.22) | copy-start | bytes 43012
  77.1 43.4 %all-to-all-start = ((s32[32,1,8]{2,1,0:T(1,128)}), s32[32,1,8]{2,1,0:T(1,128)S(1)}, u32[]{:S(2)}, u32[]{:S(2)}) async-start(s32[32,1,8]{2,1,0:T(1,128)} %bitcast.12), calls=%async_computation | async-start | bytes 32768 | tf_op jit(solution)/shard_map/all_to_all | solution.py:157
  86.9 30.2 %copy-start.8 = (s32[4]{0:T(128)S(1)}, s32[4]{0:T(128)}, u32[]{:S(2)}) copy-start(s32[4]{0:T(128)} %param.27) | copy-start | bytes 52
  86.9 30.4 %copy-start.6 = (f32[512]{0:T(512)S(1)}, f32[512]{0:T(512)}, u32[]{:S(2)}) copy-start(f32[512]{0:T(512)} %param.18) | copy-start | bytes 6148
  89.1 29.4 %copy-start.3 = (bf16[128,576]{0,1:T(8,128)(2,1)S(1)}, bf16[128,576]{0,1:T(8,128)(2,1)}, u32[]{:S(2)}) copy-start(bf16[128,576]{0,1:T(8,128)(2,1)} %pad_maximum_fusion) | copy-start | bytes 442372
  120.5 22.6 %all-to-all-start.1 = ((bf16[32,8,576]{2,1,0:T(8,128)(2,1)}), bf16[32,8,576]{2,1,0:T(8,128)(2,1)S(1)}, u32[]{:S(2)}, u32[]{:S(2)}) async-start(bf16[32,8,576]{2,1,0:T(8,128)(2,1)} %bitcast.14), calls=%async_computation.1 | async-start | bytes 655360 | tf_op jit(solution)/shard_map/all_to_all | solution.py:150
  148.4 2.9 copy-start.2
  152.4 1.6 copy-start.9
  187.2 2.1 copy-start.1
  187.2 3.1 copy-start.10
  210.1 2.1 copy-start.1
  210.1 3.1 copy-start.10
  232.9 2.1 copy-start.1
  232.9 3.1 copy-start.10
  255.7 2.1 copy-start.1
  255.7 3.1 copy-start.10
  278.5 2.1 copy-start.1
  278.5 3.1 copy-start.10
  301.3 2.1 copy-start.1
  301.4 3.1 copy-start.10
  324.2 2.1 copy-start.1
  324.2 3.1 copy-start.10
  347.0 2.1 copy-start.1
  347.0 3.1 copy-start.10
Sparse Core Ops, SparseCore 0:
  10.9 60.1 all-reduce.1
  75.0 96.3 all-gather.1
where the time goes:
time: 372 us; the launch traced here: 369 us
  matrix products  110 us (30%)
  local copies, waits for them, and re-layouts  82.8 us (22%)
  waiting for transfers between devices  80.8 us (22%)
  blocking collectives  27.5 us (7%)
  other arithmetic  24.3 us (7%)
  starting transfers between devices  19.4 us (5%)
  between operations  14.4 us (4%)
  loops' own time  9.92 us (3%)
    psum x1, waiting for transfers between devices, on_device(): lax.psum((prefill_part, decode_part), ('head', 'pool'))  60.6 us
    dot_general x8, matrix products, attend_block(): jnp.einsum('qhk,khd->qhd', expo.astype(jnp.bfloat16), values, preferred_e...  35 us
    psum x1, blocking collectives, on_device(): lax.psum((prefill_part, decode_part), ('head', 'pool'))  27.5 us
    dot_general x8, matrix products, attend_block(): jnp.dot(content, key_weight, preferred_element_type=jnp.float32)  23.1 us
    reshape x8, local copies, waits for them, and re-layouts, attend_block(): values = jnp.dot(content, value_weight, preferred_element_type=jnp.float3...  22.9 us
    dot_general x8, matrix products, attend_block(): jnp.dot(content, value_weight, preferred_element_type=jnp.float32)  21.2 us
    cond x40, local copies, waits for them, and re-layouts  18.7 us
    all_gather x1, waiting for transfers between devices, on_device(): block = lax.all_gather(latent, 'seq', axis=0, tiled=True)  15.9 us
  transfers between devices with their start and end apart: 4, of which 3 were waited for; matrix products, arithmetic and copies ran while one was open for 8% of the time, Pallas kernels for 0%

commit v1 on v0

v1 whole, which is shorter than its diff:
```python
import functools

import jax
import jax.numpy as jnp
import numpy as np
from jax import lax
from jax.experimental import pallas as pl
from jax.experimental.pallas import tpu as pltpu
from jax.sharding import PartitionSpec as P

LAT = 512
ROPE = 64
NOPE = 128
VDIM = 128
ROW = 640
TOK = 128
HALF = 64
HEADS = 16
NY, NZ = 4, 8
CHUNK = NZ * TOK
NHP = 8
SETROWS = HEADS * HALF
TQ = 512
SCALE = (NOPE + ROPE) ** (-0.5) * 1.4426950408889634
NEG = -1e30
MESH = pl.DeviceIdType.MESH
f32, bf16, i32 = jnp.float32, jnp.bfloat16, jnp.int32
NT = (((1,), (1,)), ((), ()))

UNITS = [
    [(0, 0), (1, 0), (1, 1), (1, 3), (1, 2)],
    [(0, 1), (1, 1), (0, 0), (1, 0), (1, 2)],
    [(0, 2), (0, 1), (1, 1), (0, 0), (1, 0)],
    [(0, 3), (0, 2), (0, 0), (1, 0), (0, 1)],
]
SET_CODE = [sum(s << (2 * u) for u, (s, c) in enumerate(row)) for row in UNITS]
CHUNK_CODE = [sum(c << (2 * u) for u, (s, c) in enumerate(row)) for row in UNITS]


def pick(y, table):
    return jnp.where(
        y == 0, table[0], jnp.where(y == 1, table[1], jnp.where(y == 2, table[2], table[3]))
    )


def finalize(summed, gain, freq, position):
    content = summed[:, :LAT]
    meansq = jnp.mean(content * content, -1, keepdims=True)
    content = content * lax.rsqrt(meansq + 1e-06) * gain
    tail = summed[:, LAT:]
    lane = lax.broadcasted_iota(i32, tail.shape, 1)
    angle = position * freq
    cosine, sine = jnp.cos(angle), jnp.sin(angle)
    swapped = jnp.where(lane < 32, -pltpu.roll(tail, 96, 1), pltpu.roll(tail, 32, 1))
    rotated = jnp.where(lane < ROPE, tail * cosine + swapped * sine, 0.0)
    return jnp.concatenate([content, rotated], -1).astype(bf16)


def kernel(
    hidden, down, dec_hidden, gain, freq, place_dev, place_slot, dec_query, context, key_w, value_w,
    query, cache,
    out, dec_out,
    kw, vw, q_own, q_far, kept,
    part, part_d, rs, rs_d, lat, meta, fresh,
    qa, qd, m_ref, l_ref, acc, dm, dl, dacc, sbuf, o_far, o_own,
    ld_sem, q_sems, rs_s, rs_r, rd_s, rd_r, ag_s, ag_r,
    mz_s, mz_r, my_s, my_r, z_s, z_r, y_s, y_r, f_s, f_r, sb_s, sb_r, o_sems,
):
    seq = lax.axis_index("seq")
    head = lax.axis_index("head")
    pool = lax.axis_index("pool")
    y, z = seq // NZ, seq % NZ
    hp = head * 4 + pool
    par = (z + head) % 2

    def at_hp(d):
        other = (hp + d) % NHP
        return other, {"head": other // 4, "pool": other % 4}

    def at_z(d):
        return {"seq": y * NZ + (z + d + NZ) % NZ}

    def at_y(d):
        return {"seq": (y + d + NY) % NY * NZ + z}

    partner = {"seq": (NY - 1 - y) * NZ + z}
    sibling = {"head": 1 - head}

    def remote(src, dst, ssem, rsem, dev):
        return pltpu.make_async_remote_copy(
            src_ref=src, dst_ref=dst, send_sem=ssem, recv_sem=rsem, device_id=dev,
            device_id_type=MESH,
        )

    loads = [
        pltpu.make_async_copy(query.at[pl.ds(0, HALF)], q_own, ld_sem.at[0]),
        pltpu.make_async_copy(key_w, kw, ld_sem.at[1]),
        pltpu.make_async_copy(cache, kept, ld_sem.at[2]),
        pltpu.make_async_copy(value_w, vw, ld_sem.at[3]),
    ]
    for copy in loads:
        copy.start()

    barrier = pltpu.get_barrier_semaphore()
    for d in range(1, NHP):
        pl.semaphore_signal(barrier, inc=1, device_id=at_hp(d)[1], device_id_type=MESH)
    for d in range(1, NZ):
        pl.semaphore_signal(barrier, inc=1, device_id=at_z(d), device_id_type=MESH)
    for d in range(1, NY):
        pl.semaphore_signal(barrier, inc=1, device_id=at_y(d), device_id_type=MESH)

    part[:, LAT:] = jnp.zeros((TOK, ROW - LAT), f32)
    part_d[:, LAT:] = jnp.zeros((8, ROW - LAT), f32)
    part[:, : LAT + ROPE] = jnp.dot(hidden[...], down[...], preferred_element_type=f32)
    dh = jnp.concatenate([dec_hidden[0].astype(f32), dec_hidden[1].astype(f32)], 0).astype(bf16)
    part_d[:, : LAT + ROPE] = jnp.dot(dh, down[...], preferred_element_type=f32)
    mine = meta.at[pl.ds(seq, 1)]
    meta[pl.ds(seq, 1), 0:1, :] = place_dev[...].reshape(1, 1, TOK)
    meta[pl.ds(seq, 1), 1:2, :] = place_slot[...].reshape(1, 1, TOK)

    pl.semaphore_wait(barrier, NHP + NZ + NY - 3)

    sends = []

    def go(copy):
        copy.start()
        sends.append(copy)
        return copy

    rs_copies, rd_copies = [], []
    for d in range(1, NHP):
        other, dev = at_hp(d)
        rows = pl.ds(pl.multiple_of(other * 16, 16), 16)
        rs_copies.append(
            go(remote(part.at[rows], rs.at[d - 1], rs_s.at[d - 1], rs_r.at[d - 1], dev))
        )
    mz = [
        go(remote(mine, mine, mz_s.at[d - 1], mz_r.at[d - 1], at_z(d))) for d in range(1, NZ)
    ]
    for d in range(1, NHP):
        rd_copies.append(
            go(remote(part_d, rs_d.at[d - 1], rd_s.at[d - 1], rd_r.at[d - 1], at_hp(d)[1]))
        )
    q_copy = go(remote(query.at[pl.ds(HALF, HALF)], q_far, q_sems.at[0], q_sems.at[1], partner))

    m_ref[...] = jnp.full(m_ref.shape, NEG, f32)
    l_ref[...] = jnp.zeros(l_ref.shape, f32)
    dm[...] = jnp.full(dm.shape, NEG, f32)
    dl[...] = jnp.zeros(dl.shape, f32)
    dacc[...] = jnp.zeros(dacc.shape, f32)

    def clear(i, carry):
        acc[pl.ds(pl.multiple_of(i * 256, 256), 256), :] = jnp.zeros((256, LAT), f32)
        return carry

    lax.fori_loop(0, 2 * SETROWS // 256, clear, 0)

    def absorb(load, dst, base, rows):
        def pair(j, carry):
            col = pl.multiple_of(j * 384, 128)
            t0, t1, t2 = load(col), load(col + 128), load(col + 256)
            lane = lax.broadcasted_iota(i32, t0.shape, 1)
            low = lane < 64
            nopes = (t0, pltpu.roll(jnp.where(low, t2, t1), 64, 1))
            ropes = (jnp.where(low, t1, 0.0), jnp.where(low, pltpu.roll(t2, 64, 1), 0.0))
            both = []
            for k in range(2):
                wcol = pl.multiple_of(j * 256 + k * 128, 128)
                absorbed = lax.dot_general(
                    nopes[k].astype(bf16), kw[:, pl.ds(wcol, 128)], NT, preferred_element_type=f32
                )
                both.append(jnp.concatenate([absorbed, ropes[k]], -1))
            at = pl.multiple_of(base + 2 * j * rows, 2 * rows)
            dst[pl.ds(at, 2 * rows), :] = jnp.concatenate(both, 0).astype(bf16)
            return carry

        lax.fori_loop(0, HEADS // 2, pair, 0)

    loads[0].wait()
    loads[1].wait()
    absorb(lambda c: q_own[:, pl.ds(c, 128)].astype(f32), qa, 0, HALF)
    absorb(
        lambda c: jnp.concatenate(
            [dec_query[0, :, pl.ds(c, 128)], dec_query[1, :, pl.ds(c, 128)]], 0
        ).astype(f32),
        qd, 0, 8,
    )

    for copy in rs_copies:
        copy.wait_recv()
    first = pl.multiple_of(seq * TOK + hp * 16, 16)
    summed = part[pl.ds(pl.multiple_of(hp * 16, 16), 16), :]
    for d in range(1, NHP):
        summed = summed + rs[d - 1]
    position = (first + lax.broadcasted_iota(i32, (16, 1), 0)).astype(f32)
    lat[pl.ds(first, 16), :] = finalize(summed, gain[...], freq[...], position)
    own_rows = lat.at[pl.ds(first, 16)]
    ag = [
        go(remote(own_rows, own_rows, ag_s.at[d - 1], ag_r.at[d - 1], at_hp(d)[1]))
        for d in range(1, NHP)
    ]

    for copy in mz:
        copy.wait_recv()
    plane = meta.at[pl.ds(pl.multiple_of(y * NZ, NZ), NZ)]
    my = [go(remote(plane, plane, my_s.at[d - 1], my_r.at[d - 1], at_y(d))) for d in range(1, NY)]

    for copy in ag:
        copy.wait_recv()

    def block(plane_y, b):
        return lat.at[pl.ds(pl.multiple_of((plane_y * NZ + b) * TOK, TOK), TOK)]

    def z_copy(way, k):
        step = 1 - 2 * way
        b = (z - step * (2 * k + par) + NZ) % NZ
        ref = block(y, b)
        return remote(ref, ref, z_s.at[2 * way + k], z_r.at[2 * way + k], at_z(step))

    def y_copy(way, b):
        ref = block(y, b)
        return remote(
            ref, ref, y_s.at[4 * way + b // 2], y_r.at[4 * way + b // 2], at_y(1 - 2 * way)
        )

    def sib_copy(dist, plane_y, b):
        ref = block(plane_y, b)
        return remote(
            ref, ref, sb_s.at[4 * dist + b // 2], sb_r.at[4 * dist + b // 2], sibling
        )

    def spread(b, to_sibling):
        y_copy(0, b).start()
        y_copy(1, b).start()
        if to_sibling:
            sib_copy(0, y, b).start()

    @pl.when(par == 0)
    def _():
        z_copy(0, 0).start()
        z_copy(1, 0).start()
        spread(z, False)
        z_copy(0, 0).wait_recv()
        z_copy(0, 1).start()
        z_copy(1, 0).wait_recv()
        z_copy(1, 1).start()
        spread((z + 6) % NZ, True)
        spread((z + 2) % NZ, True)
        z_copy(0, 1).wait_recv()
        spread((z + 4) % NZ, True)

    @pl.when(par == 1)
    def _():
        z_copy(0, 0).wait_recv()
        z_copy(0, 0).start()
        z_copy(1, 0).wait_recv()
        z_copy(1, 0).start()
        spread((z + 7) % NZ, True)
        spread((z + 1) % NZ, True)
        z_copy(0, 1).wait_recv()
        z_copy(0, 1).start()
        z_copy(1, 1).wait_recv()
        spread((z + 5) % NZ, True)
        spread((z + 3) % NZ, True)

    q_copy.wait_recv()
    absorb(lambda c: q_far[:, pl.ds(c, 128)].astype(f32), qa, SETROWS, HALF)

    drow = lax.broadcasted_iota(i32, (TOK, 1), 0) % 4
    dstep = lax.broadcasted_iota(i32, (TOK, 1), 0) // 4 % 2

    def decode_update(scores, mask, contents):
        scores = jnp.where(mask, scores * SCALE, NEG)
        m_old = dm[...]
        m_new = jnp.maximum(m_old, jnp.max(scores, -1, keepdims=True))
        alpha = jnp.exp2(m_old - m_new)
        dm[...] = m_new
        expo = jnp.where(mask, jnp.exp2(scores - m_new[:, :1]), 0.0)
        total = dl[...] * alpha
        for j in range(scores.shape[1] // 128):
            total = total + expo[:, 128 * j : 128 * (j + 1)]
        dl[...] = total
        dacc[...] = dacc[...] * alpha[:, :1] + jnp.dot(
            expo.astype(bf16), contents, preferred_element_type=f32
        )

    for copy in rd_copies:
        copy.wait_recv()
    summed = part_d[...]
    for d in range(1, NHP):
        summed = summed + rs_d[d - 1]
    row8 = lax.broadcasted_iota(i32, (8, 1), 0)
    ctx = [context[r] for r in range(4)]
    length = pick(row8 % 4, ctx)
    new_rows = finalize(summed, gain[...], freq[...], (length + row8 // 4).astype(f32))
    fresh[...] = jnp.concatenate([new_rows.astype(f32), jnp.zeros((TOK - 8, ROW), f32)], 0).astype(
        bf16
    )
    key = lax.broadcasted_iota(i32, (1, TOK), 1)
    decode_update(
        lax.dot_general(qd[...], fresh[...], NT, preferred_element_type=f32),
        (key < 8) & (key % 4 == drow) & (key // 4 <= dstep),
        fresh[:, :LAT],
    )

    for copy in my:
        copy.wait_recv()
    counts = jnp.zeros((16, TOK), f32)
    for b in range(NY * NZ):
        device, slot = meta[b, 0:1, :], meta[b, 1:2, :]
        here = device == seq
        high = jnp.where(here, slot // 128, -1)
        low = slot % 128
        one = lax.broadcasted_iota(i32, (16, TOK), 0) == high
        two = lax.broadcasted_iota(i32, (TOK, TOK), 0) == low
        counts = counts + lax.dot_general(
            one.astype(f32).astype(bf16), two.astype(f32).astype(bf16), NT,
            preferred_element_type=f32,
        )
    hi = lax.broadcasted_iota(i32, (16, TOK), 0)
    place = hi % 4 * 128 + lax.broadcasted_iota(i32, (16, TOK), 1)
    live = (place < pick(hi // 4, ctx)) & (counts < 0.5)
    owner = jnp.where(live, hi // 4, -1)
    loads[2].wait()
    for r in range(4):
        keyrow = jnp.concatenate([owner[4 * r + j : 4 * r + j + 1, :] for j in range(4)], 1)
        scores = lax.dot_general(
            qd[:, :LAT], kept[r, :, :LAT], NT, preferred_element_type=f32
        ) + lax.dot_general(
            qd[:, LAT : LAT + ROPE], kept[r, :, LAT:], NT, preferred_element_type=f32
        )
        decode_update(scores, keyrow == drow, kept[r, :, :LAT])

    def decode_chunk(c):
        base = pl.multiple_of(c * CHUNK, CHUNK)
        pieces = []
        for j in range(NZ):
            tile = meta[pl.ds(c * NZ + j, 1), :, :][0]
            pieces.append(jnp.where(tile[0:1] == seq, tile[1:2] // 512, -1))
        keyrow = jnp.concatenate(pieces, 1)
        scores = lax.dot_general(
            qd[...], lat[pl.ds(base, CHUNK), :], NT, preferred_element_type=f32
        )
        decode_update(scores, keyrow == drow, lat[pl.ds(base, CHUNK), :LAT])

    set_code, chunk_code = pick(y, SET_CODE), pick(y, CHUNK_CODE)

    def unit(u):
        return (set_code >> (2 * u)) & 3, (chunk_code >> (2 * u)) & 3

    def rows_of(s, t):
        return pl.ds(pl.multiple_of(s * SETROWS + t * TQ, TQ), TQ)

    def keys_of(c):
        return pl.ds(pl.multiple_of(c * CHUNK, CHUNK), CHUNK)

    def scores_into(slot, s, c, t):
        sbuf[slot] = lax.dot_general(
            qa[rows_of(s, t), :], lat[keys_of(c), :], NT, preferred_element_type=f32
        )

    def attend(slot, s, c, t):
        rows = rows_of(s, t)
        limit = jnp.where(s == 0, y, NY - 1 - y)
        start = jnp.where(c == limit, z * TOK + s * HALF, 1 << 20)
        token = start + lax.broadcasted_iota(i32, (TQ, 1), 0) % HALF
        allowed = lax.broadcasted_iota(i32, (1, CHUNK), 1) <= token
        scores = jnp.where(allowed, sbuf[slot], NEG)
        m_old = m_ref[rows, :]
        m_new = jnp.maximum(m_old, jnp.max(scores, -1, keepdims=True) * SCALE)
        alpha = jnp.exp2(m_old - m_new)
        m_ref[rows, :] = m_new
        expo = jnp.exp2(scores * SCALE - m_new[:, :1])
        total = l_ref[rows, :] * alpha
        for j in range(CHUNK // 128):
            total = total + expo[:, 128 * j : 128 * (j + 1)]
        l_ref[rows, :] = total
        acc[rows, :] = acc[rows, :] * alpha[:, :1] + jnp.dot(
            expo.astype(bf16), lat[keys_of(c), :LAT], preferred_element_type=f32
        )

    def wait_sibling(dist, plane_y):
        for k in range(4):
            b = 2 * k + 1 - head
            if dist == 0:
                pl.when(b != z)(lambda b=b: sib_copy(0, plane_y, b).wait_recv())
            else:
                sib_copy(dist, plane_y, b).wait_recv()

    def near_planes():
        below, above = (y + 3) % NY, (y + 1) % NY
        for way, plane_y in ((0, below), (1, above)):
            for k in range(4):
                b = 2 * k + head
                y_copy(way, b).wait_recv()
                if k % 2 == way:
                    far_copy(way, plane_y, b).start()
                sib_copy(1 + way, plane_y, b).start()
        wait_sibling(1, below)
        wait_sibling(2, above)

    def far_copy(way, plane_y, b):
        ref = block(plane_y, b)
        return remote(ref, ref, f_s.at[b // 2], f_r.at[b // 2], at_y(1 - 2 * way))

    def far_plane():
        plane_y = (y + 2) % NY
        for k in range(4):
            b = 2 * k + head
            far_copy(k % 2, plane_y, b).wait_recv()
            sib_copy(3, plane_y, b).start()
        wait_sibling(3, plane_y)

    wait_sibling(0, y)
    s0, c0 = unit(0)
    scores_into(0, s0, c0, 0)

    def one_unit(u, carry):
        s, c = unit(u)
        sn, cn = unit(u + 1)
        scores_into(1, s, c, 1)
        attend(0, s, c, 0)
        pl.when(((u == 0) & (y >= 2)) | ((u == 1) & (y < 2)))(near_planes)
        pl.when(((u == 2) & (y == 2)) | ((u == 3) & (y != 2)))(far_plane)
        scores_into(0, sn, cn, 0)
        attend(1, s, c, 1)
        decode_chunk((y + jnp.where(u == 0, 0, jnp.where(u == 1, 3, u - 1))) % NY)
        return carry

    lax.fori_loop(0, 4, one_unit, 0)
    s, c = unit(4)
    scores_into(1, s, c, 1)
    attend(0, s, c, 0)
    attend(1, s, c, 1)

    loads[3].wait()

    def project(base, dst):
        def one(j, carry):
            for k in range(2):
                at = pl.ds(pl.multiple_of(base + (2 * j + k) * HALF, HALF), HALF)
                col = pl.ds(pl.multiple_of((2 * j + k) * VDIM, VDIM), VDIM)
                total = jnp.sum(l_ref[at, :], -1, keepdims=True)
                mixed = (acc[at, :] / total).astype(bf16)
                dst[:, col] = jnp.dot(mixed, vw[:, col], preferred_element_type=f32).astype(bf16)
            return carry

        lax.fori_loop(0, HEADS // 2, one, 0)

    project(SETROWS, o_far)
    home = go(remote(o_far, out.at[pl.ds(HALF, HALF)], o_sems.at[0], o_sems.at[1], partner))
    project(0, o_own)
    keep = pltpu.make_async_copy(o_own, out.at[pl.ds(0, HALF)], o_sems.at[2])
    keep.start()
    dmixed = dacc[...] / jnp.sum(dl[...], -1, keepdims=True)
    for h in range(HEADS):
        col = slice(h * VDIM, (h + 1) * VDIM)
        res = jnp.dot(
            dmixed[8 * h : 8 * h + 8].astype(bf16), vw[:, col], preferred_element_type=f32
        ).astype(bf16)
        dec_out[0, :, col] = res[0:4]
        dec_out[1, :, col] = res[4:8]

    for copy in sends:
        copy.wait_send()
    for way in range(2):
        z_copy(way, 0).wait_send()
        for k in range(4):
            y_copy(way, 2 * k + head).wait_send()
    z_copy(0, 1).wait_send()
    pl.when(par == 0)(lambda: z_copy(1, 1).wait_send())
    for k in range(4):
        b = 2 * k + head
        far_copy(k % 2, (y + 3 + 2 * (k % 2)) % NY, b).wait_send()
        pl.when(b != z)(lambda b=b: sib_copy(0, y, b).wait_send())
        sib_copy(1, (y + 3) % NY, b).wait_send()
        sib_copy(2, (y + 1) % NY, b).wait_send()
        sib_copy(3, (y + 2) % NY, b).wait_send()
    keep.wait()
    home.wait_recv()


def on_device(
    prefill_hidden, down_weight, latent_gain, key_weight, value_weight, prefill_query,
    decode_hidden, decode_query, latent_cache, place_device, place_slot, context_length,
):
    half = ROPE // 2
    freq = 10000.0 ** (-(np.arange(128) % half).astype(np.float64) / half)
    freq = jnp.asarray(freq.astype(np.float32)[None])
    vmem = pl.BlockSpec(memory_space=pltpu.VMEM)
    hbm = pl.BlockSpec(memory_space=pl.ANY)
    dma = pltpu.SemaphoreType.DMA
    return pl.pallas_call(
        kernel,
        out_shape=(
            jax.ShapeDtypeStruct((TOK, HEADS * VDIM), bf16),
            jax.ShapeDtypeStruct((2, 4, HEADS * VDIM), bf16),
        ),
        in_specs=[vmem] * 8 + [pl.BlockSpec(memory_space=pltpu.SMEM)] + [hbm] * 4,
        out_specs=(hbm, vmem),
        scratch_shapes=[
            pltpu.VMEM((LAT, HEADS * NOPE), bf16),
            pltpu.VMEM((LAT, HEADS * VDIM), bf16),
            pltpu.VMEM((HALF, HEADS * 192), bf16),
            pltpu.VMEM((HALF, HEADS * 192), bf16),
            pltpu.VMEM((4, 512, LAT + ROPE), bf16),
            pltpu.VMEM((TOK, ROW), f32),
            pltpu.VMEM((8, ROW), f32),
            pltpu.VMEM((NHP - 1, 16, ROW), f32),
            pltpu.VMEM((NHP - 1, 8, ROW), f32),
            pltpu.VMEM((NY * CHUNK, ROW), bf16),
            pltpu.VMEM((NY * NZ, 8, TOK), i32),
            pltpu.VMEM((TOK, ROW), bf16),
            pltpu.VMEM((2 * SETROWS, ROW), bf16),
            pltpu.VMEM((TOK, ROW), bf16),
            pltpu.VMEM((2 * SETROWS, 128), f32),
            pltpu.VMEM((2 * SETROWS, 128), f32),
            pltpu.VMEM((2 * SETROWS, LAT), f32),
            pltpu.VMEM((TOK, 128), f32),
            pltpu.VMEM((TOK, 128), f32),
            pltpu.VMEM((TOK, LAT), f32),
            pltpu.VMEM((2, TQ, CHUNK), f32),
            pltpu.VMEM((HALF, HEADS * VDIM), bf16),
            pltpu.VMEM((HALF, HEADS * VDIM), bf16),
            dma((4,)), dma((2,)),
            dma((7,)), dma((7,)), dma((7,)), dma((7,)), dma((7,)), dma((7,)),
            dma((7,)), dma((7,)), dma((3,)), dma((3,)),
            dma((4,)), dma((4,)), dma((8,)), dma((8,)), dma((4,)), dma((4,)),
            dma((16,)), dma((16,)), dma((3,)),
        ],
        compiler_params=pltpu.CompilerParams(
            collective_id=0, has_side_effects=True, vmem_limit_bytes=56 << 20
        ),
    )(
        prefill_hidden, down_weight, decode_hidden, latent_gain.reshape(1, LAT), freq,
        place_device.reshape(1, TOK), place_slot.reshape(1, TOK), decode_query, context_length,
        key_weight, value_weight, prefill_query, latent_cache,
    )


def solution(mesh):
    in_specs = (
        P("seq", ("head", "pool")),
        P(("head", "pool"), None),
        P(),
        P(None, ("head", "pool")),
        P(None, ("head", "pool")),
        P("seq", ("head", "pool")),
        P(None, "seq", ("head", "pool")),
        P(None, "seq", ("head", "pool")),
        P("seq", None, None),
        P("seq"),
        P("seq"),
        P("seq"),
    )
    out_specs = (P("seq", ("head", "pool")), P(None, "seq", ("head", "pool")))
    return jax.shard_map(
        on_device, mesh=mesh, in_specs=in_specs, out_specs=out_specs, check_vma=False
    )
```

time: 372 us -> 94.7 us (0.25)
  the two profiles are of different devices: /device:TPU:252 before, /device:TPU:24 now
where the time goes in v1:
time: 94.7 us; the launch traced here: 94 us
  Pallas kernels  83.4 us (88%)
  local copies, waits for them, and re-layouts  9.96 us (11%)
    pallas_call x1, Pallas kernels, on_device(): pl.pallas_call(kernel, out_shape=(jax.ShapeDtypeStruct((TOK, HEADS * VDIM...  83.4 us
    unnamed x4, local copies, waits for them, and re-layouts  9.96 us

profile of v1, /device:TPU:24, one launch (start us, length us, event | category | flops | bytes accessed | tf_op | source)
XLA Modules:
  0.0 94.0 jit_solution(15078022802159148439)
XLA Ops:
  0.6 2.4 %copy.15.down = bf16[896,576]{1,0:T(8,128)(2,1)} copy(bf16[896,576]{0,1:T(8,128)(2,1)} %param.14) | data formatting | bytes 2064384 | tf_op args[1]
  3.0 4.3 %copy.16.cache = bf16[4,512,576]{2,1,0:T(8,128)(2,1)} copy(bf16[4,512,576]{1,2,0:T(8,128)(2,1)} %param.21) | data formatting | bytes 4718592 | tf_op args[8]
  7.3 83.4 %shard_map.140 = (bf16[128,2048]{1,0:T(8,128)(2,1)}, bf16[2,4,2048]{2,1,0:T(4,128)(2,1)}) custom-call(bf16[128,896]{1,0:T(8,128)(2,1)} %hidden.1, bf16[896,576]{1,0:T(8,128)(2,1)} %copy.15.down, bf16[2,4,896]{2,1,0:T(4,128)(2,1)} %dec_hidden.1, f32[1,512]{1,0:T(1,128)} %bitcast.3, f32[1,128]{1,0:T(1,128)} %constant.2.clone.freq, s32[1,128]{1,0:T(1,128)} %bitcast.4, ...), custom_call_target="tpu_custom_call" | custom-call | tf_op jit(solution)/shard_map/pallas_call | solution.py:493
  90.8 1.9 %copy.19 = bf16[128,2048]{1,0:T(8,128)(2,1)} copy(bf16[128,2048]{1,0:T(8,128)(2,1)} %get-tuple-element.4) | data formatting | bytes 1048576
  92.7 1.4 %copy.20 = bf16[2,4,2048]{2,1,0:T(4,128)(2,1)} copy(bf16[2,4,2048]{2,1,0:T(4,128)(2,1)} %get-tuple-element.5) | data formatting | bytes 65536

commit v2 on v1

--- a/solution.py
+++ b/solution.py
@@ -19,6 +19,7 @@
 NY, NZ = 4, 8
 CHUNK = NZ * TOK
 NHP = 8
+OWN, FAR = 2, 5
 SETROWS = HEADS * HALF
 TQ = 512
 SCALE = (NOPE + ROPE) ** (-0.5) * 1.4426950408889634
@@ -57,21 +58,22 @@
 
 
 def kernel(
-    hidden, down, dec_hidden, gain, freq, place_dev, place_slot, dec_query, context, key_w, value_w,
-    query, cache,
+    hidden_in, down_in, dec_hidden_in, gain_in, freq_in, dev_in, slot_in, dec_query_in, context,
+    key_w, value_w, query, cache,
     out, dec_out,
+    hidden, down, dec_hidden, gain, freq, place_dev, place_slot, dec_query,
     kw, vw, q_own, q_far, kept,
     part, part_d, rs, rs_d, lat, meta, fresh,
     qa, qd, m_ref, l_ref, acc, dm, dl, dacc, sbuf, o_far, o_own,
-    ld_sem, q_sems, rs_s, rs_r, rd_s, rd_r, ag_s, ag_r,
-    mz_s, mz_r, my_s, my_r, z_s, z_r, y_s, y_r, f_s, f_r, sb_s, sb_r, o_sems,
+    ld_sem, q_sems, rs_s, rs_r, rd_s, rd_r, mz_s, mz_r, my_s, my_r,
+    ax_s, ax_r, fz_s, fz_r, nz_s, nz_r, xf_s, xf_r, yf_s, yf_r, yn_s, yn_r, fw_s, fw_r,
+    sb_s, sb_r, o_sems,
 ):
     seq = lax.axis_index("seq")
     head = lax.axis_index("head")
     pool = lax.axis_index("pool")
     y, z = seq // NZ, seq % NZ
     hp = head * 4 + pool
-    par = (z + head) % 2
 
     def at_hp(d):
         other = (hp + d) % NHP
@@ -82,6 +84,9 @@
 
     def at_y(d):
         return {"seq": (y + d + NY) % NY * NZ + z}
+
+    def at_x(d):
+        return {"pool": (pool + d) % 4}
 
     partner = {"seq": (NY - 1 - y) * NZ + z}
     sibling = {"head": 1 - head}
@@ -92,13 +97,23 @@
             device_id_type=MESH,
         )
 
+    first_loads = [
+        pltpu.make_async_copy(src, dst, ld_sem.at[4 + i])
+        for i, (src, dst) in enumerate(
+            (
+                (hidden_in, hidden), (down_in, down), (dec_hidden_in, dec_hidden),
+                (dev_in, place_dev), (slot_in, place_slot), (gain_in, gain), (freq_in, freq),
+                (dec_query_in, dec_query),
+            )
+        )
+    ]
     loads = [
         pltpu.make_async_copy(query.at[pl.ds(0, HALF)], q_own, ld_sem.at[0]),
         pltpu.make_async_copy(key_w, kw, ld_sem.at[1]),
         pltpu.make_async_copy(cache, kept, ld_sem.at[2]),
         pltpu.make_async_copy(value_w, vw, ld_sem.at[3]),
     ]
-    for copy in loads:
+    for copy in first_loads + loads:
         copy.start()
 
     barrier = pltpu.get_barrier_semaphore()
@@ -109,11 +124,15 @@
     for d in range(1, NY):
         pl.semaphore_signal(barrier, inc=1, device_id=at_y(d), device_id_type=MESH)
 
+    for copy in first_loads:
+        copy.wait()
     part[:, LAT:] = jnp.zeros((TOK, ROW - LAT), f32)
     part_d[:, LAT:] = jnp.zeros((8, ROW - LAT), f32)
-    part[:, : LAT + ROPE] = jnp.dot(hidden[...], down[...], preferred_element_type=f32)
+    part[:, : LAT + ROPE] = lax.dot_general(
+        hidden[...], down[...], NT, preferred_element_type=f32
+    )
     dh = jnp.concatenate([dec_hidden[0].astype(f32), dec_hidden[1].astype(f32)], 0).astype(bf16)
-    part_d[:, : LAT + ROPE] = jnp.dot(dh, down[...], preferred_element_type=f32)
+    part_d[:, : LAT + ROPE] = lax.dot_general(dh, down[...], NT, preferred_element_type=f32)
     mine = meta.at[pl.ds(seq, 1)]
     meta[pl.ds(seq, 1), 0:1, :] = place_dev[...].reshape(1, 1, TOK)
     meta[pl.ds(seq, 1), 1:2, :] = place_slot[...].reshape(1, 1, TOK)
@@ -137,10 +156,6 @@
     mz = [
         go(remote(mine, mine, mz_s.at[d - 1], mz_r.at[d - 1], at_z(d))) for d in range(1, NZ)
     ]
-    for d in range(1, NHP):
-        rd_copies.append(
-            go(remote(part_d, rs_d.at[d - 1], rd_s.at[d - 1], rd_r.at[d - 1], at_hp(d)[1]))
-        )
     q_copy = go(remote(query.at[pl.ds(HALF, HALF)], q_far, q_sems.at[0], q_sems.at[1], partner))
 
     m_ref[...] = jnp.full(m_ref.shape, NEG, f32)
@@ -188,88 +203,90 @@
 
     for copy in rs_copies:
         copy.wait_recv()
-    first = pl.multiple_of(seq * TOK + hp * 16, 16)
+    first = seq * TOK + hp * 16
     summed = part[pl.ds(pl.multiple_of(hp * 16, 16), 16), :]
     for d in range(1, NHP):
         summed = summed + rs[d - 1]
     position = (first + lax.broadcasted_iota(i32, (16, 1), 0)).astype(f32)
-    lat[pl.ds(first, 16), :] = finalize(summed, gain[...], freq[...], position)
-    own_rows = lat.at[pl.ds(first, 16)]
-    ag = [
-        go(remote(own_rows, own_rows, ag_s.at[d - 1], ag_r.at[d - 1], at_hp(d)[1]))
-        for d in range(1, NHP)
+    lat[y, OWN, hp] = finalize(summed, gain[...], freq[...], position)
+
+    half = pl.ds(head * 4, 4)
+    own_rows = lat.at[y, OWN, hp]
+    ax = [
+        go(remote(own_rows, own_rows, ax_s.at[d - 1], ax_r.at[d - 1], at_x(d))) for d in (1, 2, 3)
     ]
+    fz = []
+    for k, d in enumerate((3, 4, 5)):
+        there = lat.at[y, (OWN - d) % NZ, hp]
+        fz.append(go(remote(own_rows, there, fz_s.at[k], fz_r.at[k], at_z(d))))
+    for d in range(1, NHP):
+        rd_copies.append(
+            go(remote(part_d, rs_d.at[d - 1], rd_s.at[d - 1], rd_r.at[d - 1], at_hp(d)[1]))
+        )
+
+    for copy in ax:
+        copy.wait_recv()
+    own_half = lat.at[y, OWN, half]
+    nz = {}
+    for k, d in enumerate((1, -1, 2, -2)):
+        there = lat.at[y, OWN - d, half]
+        nz[d] = go(remote(own_half, there, nz_s.at[k], nz_r.at[k], at_z(d)))
+
+    def to_planes(i):
+        ref = lat.at[y, i, half]
+        for w, d in enumerate((1, -1)):
+            yn[d].append(go(remote(ref, ref, yn_s.at[5 * w + i], yn_r.at[5 * w + i], at_y(d))))
+
+    yn = {1: [], -1: []}
+    to_planes(OWN)
 
     for copy in mz:
         copy.wait_recv()
     plane = meta.at[pl.ds(pl.multiple_of(y * NZ, NZ), NZ)]
     my = [go(remote(plane, plane, my_s.at[d - 1], my_r.at[d - 1], at_y(d))) for d in range(1, NY)]
 
-    for copy in ag:
-        copy.wait_recv()
-
-    def block(plane_y, b):
-        return lat.at[pl.ds(pl.multiple_of((plane_y * NZ + b) * TOK, TOK), TOK)]
-
-    def z_copy(way, k):
-        step = 1 - 2 * way
-        b = (z - step * (2 * k + par) + NZ) % NZ
-        ref = block(y, b)
-        return remote(ref, ref, z_s.at[2 * way + k], z_r.at[2 * way + k], at_z(step))
-
-    def y_copy(way, b):
-        ref = block(y, b)
-        return remote(
-            ref, ref, y_s.at[4 * way + b // 2], y_r.at[4 * way + b // 2], at_y(1 - 2 * way)
-        )
-
-    def sib_copy(dist, plane_y, b):
-        ref = block(plane_y, b)
-        return remote(
-            ref, ref, sb_s.at[4 * dist + b // 2], sb_r.at[4 * dist + b // 2], sibling
-        )
-
-    def spread(b, to_sibling):
-        y_copy(0, b).start()
-        y_copy(1, b).start()
-        if to_sibling:
-            sib_copy(0, y, b).start()
-
-    @pl.when(par == 0)
-    def _():
-        z_copy(0, 0).start()
-        z_copy(1, 0).start()
-        spread(z, False)
-        z_copy(0, 0).wait_recv()
-        z_copy(0, 1).start()
-        z_copy(1, 0).wait_recv()
-        z_copy(1, 1).start()
-        spread((z + 6) % NZ, True)
-        spread((z + 2) % NZ, True)
-        z_copy(0, 1).wait_recv()
-        spread((z + 4) % NZ, True)
-
-    @pl.when(par == 1)
-    def _():
-        z_copy(0, 0).wait_recv()
-        z_copy(0, 0).start()
-        z_copy(1, 0).wait_recv()
-        z_copy(1, 0).start()
-        spread((z + 7) % NZ, True)
-        spread((z + 1) % NZ, True)
-        z_copy(0, 1).wait_recv()
-        z_copy(0, 1).start()
-        z_copy(1, 1).wait_recv()
-        spread((z + 5) % NZ, True)
-        spread((z + 3) % NZ, True)
+    def over_x(dist, plane_y):
+        ref = lat.at[plane_y, pl.ds(FAR, 3), hp]
+        return [
+            go(
+                remote(
+                    ref, ref, xf_s.at[3 * dist + d - 1], xf_r.at[3 * dist + d - 1], at_x(d)
+                )
+            )
+            for d in (1, 2, 3)
+        ]
+
+    for copy in fz:
+        copy.wait_recv()
+    xf = [over_x(0, y)]
+    far_rows = lat.at[y, pl.ds(FAR, 3), hp]
+    yf = [go(remote(far_rows, far_rows, yf_s.at[d - 1], yf_r.at[d - 1], at_y(d))) for d in (1, 2, 3)]
+
+    def to_sibling(k, plane_y, start, count):
+        ref = lat.at[plane_y, pl.ds(start, count), half]
+        return remote(ref, ref, sb_s.at[k], sb_r.at[k], sibling)
+
+    def from_sibling(k, plane_y, start, count):
+        to_sibling(k, plane_y, start, count).wait_recv()
 
     q_copy.wait_recv()
     absorb(lambda c: q_far[:, pl.ds(c, 128)].astype(f32), qa, SETROWS, HALF)
 
+    for d in (1, -1, 2, -2):
+        nz[d].wait_recv()
+        to_planes(OWN - d)
+    to_sibling(0, y, 0, 5).start()
+    for d in (1, 2, 3):
+        yf[d - 1].wait_recv()
+        xf.append(over_x(d, (y - d + NY) % NY))
+    for copy in xf[0]:
+        copy.wait_recv()
+    to_sibling(1, y, FAR, 3).start()
+
     drow = lax.broadcasted_iota(i32, (TOK, 1), 0) % 4
     dstep = lax.broadcasted_iota(i32, (TOK, 1), 0) // 4 % 2
 
-    def decode_update(scores, mask, contents):
+    def decode_update(scores, mask, contents, dims=(((1,), (0,)), ((), ()))):
         scores = jnp.where(mask, scores * SCALE, NEG)
         m_old = dm[...]
         m_new = jnp.maximum(m_old, jnp.max(scores, -1, keepdims=True))
@@ -280,8 +297,8 @@
         for j in range(scores.shape[1] // 128):
             total = total + expo[:, 128 * j : 128 * (j + 1)]
         dl[...] = total
-        dacc[...] = dacc[...] * alpha[:, :1] + jnp.dot(
-            expo.astype(bf16), contents, preferred_element_type=f32
+        dacc[...] = dacc[...] * alpha[:, :1] + lax.dot_general(
+            expo.astype(bf16), contents, dims, preferred_element_type=f32
         )
 
     for copy in rd_copies:
@@ -324,24 +341,21 @@
     loads[2].wait()
     for r in range(4):
         keyrow = jnp.concatenate([owner[4 * r + j : 4 * r + j + 1, :] for j in range(4)], 1)
-        scores = lax.dot_general(
-            qd[:, :LAT], kept[r, :, :LAT], NT, preferred_element_type=f32
-        ) + lax.dot_general(
-            qd[:, LAT : LAT + ROPE], kept[r, :, LAT:], NT, preferred_element_type=f32
-        )
-        decode_update(scores, keyrow == drow, kept[r, :, :LAT])
+        scores = jnp.dot(qd[:, :LAT], kept[r, :LAT], preferred_element_type=f32) + jnp.dot(
+            qd[:, LAT : LAT + ROPE], kept[r, LAT:], preferred_element_type=f32
+        )
+        decode_update(scores, keyrow == drow, kept[r, :LAT], NT)
 
     def decode_chunk(c):
-        base = pl.multiple_of(c * CHUNK, CHUNK)
         pieces = []
         for j in range(NZ):
-            tile = meta[pl.ds(c * NZ + j, 1), :, :][0]
+            tile = meta[pl.ds(c * NZ + (z + j + 6) % NZ, 1), :, :][0]
             pieces.append(jnp.where(tile[0:1] == seq, tile[1:2] // 512, -1))
         keyrow = jnp.concatenate(pieces, 1)
         scores = lax.dot_general(
-            qd[...], lat[pl.ds(base, CHUNK), :], NT, preferred_element_type=f32
-        )
-        decode_update(scores, keyrow == drow, lat[pl.ds(base, CHUNK), :LAT])
+            qd[...], lat[c].reshape(CHUNK, ROW), NT, preferred_element_type=f32
+        )
+        decode_update(scores, keyrow == drow, lat[c, :, :, :, :LAT].reshape(CHUNK, LAT))
 
     set_code, chunk_code = pick(y, SET_CODE), pick(y, CHUNK_CODE)
 
@@ -351,12 +365,9 @@
     def rows_of(s, t):
         return pl.ds(pl.multiple_of(s * SETROWS + t * TQ, TQ), TQ)
 
-    def keys_of(c):
-        return pl.ds(pl.multiple_of(c * CHUNK, CHUNK), CHUNK)
-
     def scores_into(slot, s, c, t):
         sbuf[slot] = lax.dot_general(
-            qa[rows_of(s, t), :], lat[keys_of(c), :], NT, preferred_element_type=f32
+            qa[rows_of(s, t), :], lat[c].reshape(CHUNK, ROW), NT, preferred_element_type=f32
         )
 
     def attend(slot, s, c, t):
@@ -364,7 +375,8 @@
         limit = jnp.where(s == 0, y, NY - 1 - y)
         start = jnp.where(c == limit, z * TOK + s * HALF, 1 << 20)
         token = start + lax.broadcasted_iota(i32, (TQ, 1), 0) % HALF
-        allowed = lax.broadcasted_iota(i32, (1, CHUNK), 1) <= token
+        key = (lax.broadcasted_iota(i32, (1, CHUNK), 1) + (z + 6) * TOK) & (CHUNK - 1)
+        allowed = key <= token
         scores = jnp.where(allowed, sbuf[slot], NEG)
         m_old = m_ref[rows, :]
         m_new = jnp.maximum(m_old, jnp.max(scores, -1, keepdims=True) * SCALE)
@@ -376,42 +388,43 @@
             total = total + expo[:, 128 * j : 128 * (j + 1)]
         l_ref[rows, :] = total
         acc[rows, :] = acc[rows, :] * alpha[:, :1] + jnp.dot(
-            expo.astype(bf16), lat[keys_of(c), :LAT], preferred_element_type=f32
-        )
-
-    def wait_sibling(dist, plane_y):
-        for k in range(4):
-            b = 2 * k + 1 - head
-            if dist == 0:
-                pl.when(b != z)(lambda b=b: sib_copy(0, plane_y, b).wait_recv())
-            else:
-                sib_copy(dist, plane_y, b).wait_recv()
+            expo.astype(bf16), lat[c, :, :, :, :LAT].reshape(CHUNK, LAT), preferred_element_type=f32
+        )
+
+    below, above, across = (y + 3) % NY, (y + 1) % NY, (y + 2) % NY
+
+    def forward(w):
+        ref = lat.at[(below, above)[w], pl.ds(2 * w, 2 + w), half]
+        return remote(ref, ref, fw_s.at[w], fw_r.at[w], at_y(1 - 2 * w))
+
+    def forwarded(w):
+        ref = lat.at[across, pl.ds(2 * w, 2 + w), half]
+        return remote(ref, ref, fw_s.at[w], fw_r.at[w], at_y(1 - 2 * w))
 
     def near_planes():
-        below, above = (y + 3) % NY, (y + 1) % NY
-        for way, plane_y in ((0, below), (1, above)):
-            for k in range(4):
-                b = 2 * k + head
-                y_copy(way, b).wait_recv()
-                if k % 2 == way:
-                    far_copy(way, plane_y, b).start()
-                sib_copy(1 + way, plane_y, b).start()
-        wait_sibling(1, below)
-        wait_sibling(2, above)
-
-    def far_copy(way, plane_y, b):
-        ref = block(plane_y, b)
-        return remote(ref, ref, f_s.at[b // 2], f_r.at[b // 2], at_y(1 - 2 * way))
+        for w, (d, plane_y) in enumerate(((1, below), (-1, above))):
+            for copy in yn[d]:
+                copy.wait_recv()
+            forward(w).start()
+            to_sibling(2 + 2 * w, plane_y, 0, 5).start()
+        for w, (dist, plane_y) in enumerate(((1, below), (3, above))):
+            for copy in xf[dist]:
+                copy.wait_recv()
+            to_sibling(3 + 2 * w, plane_y, FAR, 3).start()
+        for w, plane_y in enumerate((below, above)):
+            from_sibling(2 + 2 * w, plane_y, 0, 5)
+            from_sibling(3 + 2 * w, plane_y, FAR, 3)
 
     def far_plane():
-        plane_y = (y + 2) % NY
-        for k in range(4):
-            b = 2 * k + head
-            far_copy(k % 2, plane_y, b).wait_recv()
-            sib_copy(3, plane_y, b).start()
-        wait_sibling(3, plane_y)
-
-    wait_sibling(0, y)
+        for w in range(2):
+            forwarded(w).wait_recv()
+        for copy in xf[2]:
+            copy.wait_recv()
+        to_sibling(6, across, 0, NZ).start()
+        from_sibling(6, across, 0, NZ)
+
+    from_sibling(0, y, 0, 5)
+    from_sibling(1, y, FAR, 3)
     s0, c0 = unit(0)
     scores_into(0, s0, c0, 0)
 
@@ -463,19 +476,13 @@
 
     for copy in sends:
         copy.wait_send()
-    for way in range(2):
-        z_copy(way, 0).wait_send()
-        for k in range(4):
-            y_copy(way, 2 * k + head).wait_send()
-    z_copy(0, 1).wait_send()
-    pl.when(par == 0)(lambda: z_copy(1, 1).wait_send())
-    for k in range(4):
-        b = 2 * k + head
-        far_copy(k % 2, (y + 3 + 2 * (k % 2)) % NY, b).wait_send()
-        pl.when(b != z)(lambda b=b: sib_copy(0, y, b).wait_send())
-        sib_copy(1, (y + 3) % NY, b).wait_send()
-        sib_copy(2, (y + 1) % NY, b).wait_send()
-        sib_copy(3, (y + 2) % NY, b).wait_send()
+    for w in range(2):
+        forward(w).wait_send()
+        to_sibling(2 + 2 * w, (below, above)[w], 0, 5).wait_send()
+        to_sibling(3 + 2 * w, (below, above)[w], FAR, 3).wait_send()
+    to_sibling(0, y, 0, 5).wait_send()
+    to_sibling(1, y, FAR, 3).wait_send()
+    to_sibling(6, across, 0, NZ).wait_send()
     keep.wait()
     home.wait_recv()
 
@@ -496,19 +503,27 @@
             jax.ShapeDtypeStruct((TOK, HEADS * VDIM), bf16),
             jax.ShapeDtypeStruct((2, 4, HEADS * VDIM), bf16),
         ),
-        in_specs=[vmem] * 8 + [pl.BlockSpec(memory_space=pltpu.SMEM)] + [hbm] * 4,
+        in_specs=[hbm] * 8 + [pl.BlockSpec(memory_space=pltpu.SMEM)] + [hbm] * 4,
         out_specs=(hbm, vmem),
         scratch_shapes=[
+            pltpu.VMEM((TOK, 896), bf16),
+            pltpu.VMEM((LAT + ROPE, 896), bf16),
+            pltpu.VMEM((2, 4, 896), bf16),
+            pltpu.VMEM((1, LAT), f32),
+            pltpu.VMEM((1, 128), f32),
+            pltpu.VMEM((1, TOK), i32),
+            pltpu.VMEM((1, TOK), i32),
+            pltpu.VMEM((2, 4, HEADS * 192), bf16),
             pltpu.VMEM((LAT, HEADS * NOPE), bf16),
             pltpu.VMEM((LAT, HEADS * VDIM), bf16),
             pltpu.VMEM((HALF, HEADS * 192), bf16),
             pltpu.VMEM((HALF, HEADS * 192), bf16),
-            pltpu.VMEM((4, 512, LAT + ROPE), bf16),
+            pltpu.VMEM((4, LAT + ROPE, 512), bf16),
             pltpu.VMEM((TOK, ROW), f32),
             pltpu.VMEM((8, ROW), f32),
             pltpu.VMEM((NHP - 1, 16, ROW), f32),
             pltpu.VMEM((NHP - 1, 8, ROW), f32),
-            pltpu.VMEM((NY * CHUNK, ROW), bf16),
+            pltpu.VMEM((NY, NZ, NHP, 16, ROW), bf16),
             pltpu.VMEM((NY * NZ, 8, TOK), i32),
             pltpu.VMEM((TOK, ROW), bf16),
             pltpu.VMEM((2 * SETROWS, ROW), bf16),
@@ -522,19 +537,19 @@
             pltpu.VMEM((2, TQ, CHUNK), f32),
             pltpu.VMEM((HALF, HEADS * VDIM), bf16),
             pltpu.VMEM((HALF, HEADS * VDIM), bf16),
-            dma((4,)), dma((2,)),
-            dma((7,)), dma((7,)), dma((7,)), dma((7,)), dma((7,)), dma((7,)),
+            dma((12,)), dma((2,)), dma((7,)), dma((7,)), dma((7,)), dma((7,)),
             dma((7,)), dma((7,)), dma((3,)), dma((3,)),
-            dma((4,)), dma((4,)), dma((8,)), dma((8,)), dma((4,)), dma((4,)),
-            dma((16,)), dma((16,)), dma((3,)),
+            dma((3,)), dma((3,)), dma((3,)), dma((3,)), dma((4,)), dma((4,)),
+            dma((12,)), dma((12,)), dma((3,)), dma((3,)), dma((10,)), dma((10,)),
+            dma((2,)), dma((2,)), dma((7,)), dma((7,)), dma((3,)),
         ],
         compiler_params=pltpu.CompilerParams(
             collective_id=0, has_side_effects=True, vmem_limit_bytes=56 << 20
         ),
     )(
-        prefill_hidden, down_weight, decode_hidden, latent_gain.reshape(1, LAT), freq,
+        prefill_hidden, down_weight.T, decode_hidden, latent_gain.reshape(1, LAT), freq,
         place_device.reshape(1, TOK), place_slot.reshape(1, TOK), decode_query, context_length,
-        key_weight, value_weight, prefill_query, latent_cache,
+        key_weight, value_weight, prefill_query, latent_cache.transpose(0, 2, 1),
     )
 
 

time: 94.7 us -> 74.3 us (0.78)
  Pallas kernels: 83.4 us -> 70.1 us
  local copies, waits for them, and re-layouts: 9.96 us -> 3.27 us
    pallas_call x1, Pallas kernels: 83.4 us -> 70.1 us  [on_device(): pl.pallas_call(kernel, out_shape=(jax.ShapeDtypeStruct((TOK, HEADS * VDIM...]
    unnamed x4 -> x2, local copies, waits for them, and re-layouts: 9.96 us -> 3.27 us
where the time goes in v2:
time: 74.3 us; the launch traced here: 74 us
  Pallas kernels  70.1 us (94%)
  local copies, waits for them, and re-layouts  3.27 us (4%)
    pallas_call x1, Pallas kernels, on_device(): pl.pallas_call(kernel, out_shape=(jax.ShapeDtypeStruct((TOK, HEADS * VDIM...  70.1 us
    unnamed x2, local copies, waits for them, and re-layouts  3.27 us

profile of v2, /device:TPU:24, one launch (start us, length us, event | category | flops | bytes accessed | tf_op | source)
XLA Modules:
  0.0 74.0 jit_solution(1613027175420004140)
XLA Ops:
  0.6 70.1 %shard_map.140 = (bf16[128,2048]{1,0:T(8,128)(2,1)}, bf16[2,4,2048]{2,1,0:T(4,128)(2,1)}) custom-call(bf16[128,896]{1,0:T(8,128)(2,1)} %hidden_in.1, bf16[576,896]{1,0:T(8,128)(2,1)} %bitcast.6, bf16[2,4,896]{2,1,0:T(4,128)(2,1)} %dec_hidden_in.1, f32[1,512]{1,0:T(1,128)} %bitcast.7, f32[1,128]{1,0:T(1,128)} %constant.2.clone.freq_in, s32[1,128]{1,0:T(1,128)} %bitcast.8, ...), custom_call_target="tpu_custom_call" | custom-call | tf_op jit(solution)/shard_map/pallas_call | solution.py:500
  70.8 1.9 %copy.17 = bf16[128,2048]{1,0:T(8,128)(2,1)} copy(bf16[128,2048]{1,0:T(8,128)(2,1)} %get-tuple-element.4) | data formatting | bytes 1048576
  72.7 1.4 %copy.18 = bf16[2,4,2048]{2,1,0:T(4,128)(2,1)} copy(bf16[2,4,2048]{2,1,0:T(4,128)(2,1)} %get-tuple-element.5) | data formatting | bytes 65536

commit v3 on v2

--- a/solution.py
+++ b/solution.py
@@ -14,28 +14,28 @@
 VDIM = 128
 ROW = 640
 TOK = 128
-HALF = 64
 HEADS = 16
 NY, NZ = 4, 8
 CHUNK = NZ * TOK
 NHP = 8
 OWN, FAR = 2, 5
-SETROWS = HEADS * HALF
 TQ = 512
+GUEST = 4
+GUEST_COL = 12
 SCALE = (NOPE + ROPE) ** (-0.5) * 1.4426950408889634
 NEG = -1e30
 MESH = pl.DeviceIdType.MESH
 f32, bf16, i32 = jnp.float32, jnp.bfloat16, jnp.int32
 NT = (((1,), (1,)), ((), ()))
 
-UNITS = [
-    [(0, 0), (1, 0), (1, 1), (1, 3), (1, 2)],
-    [(0, 1), (1, 1), (0, 0), (1, 0), (1, 2)],
-    [(0, 2), (0, 1), (1, 1), (0, 0), (1, 0)],
-    [(0, 3), (0, 2), (0, 0), (1, 0), (0, 1)],
+STEPS = [
+    [(0, 0), (1, 0), (2, 0), (3, 0), (0, 0), (0, 1), (0, 3), (0, 2)],
+    [(t, c) for c in (1, 0) for t in range(4)],
+    [(t, c) for c in (2, 1, 0) for t in range(4)],
+    [(t, c) for c in (3, 2, 0, 1) for t in range(3)],
 ]
-SET_CODE = [sum(s << (2 * u) for u, (s, c) in enumerate(row)) for row in UNITS]
-CHUNK_CODE = [sum(c << (2 * u) for u, (s, c) in enumerate(row)) for row in UNITS]
+TILE_CODE = [sum(t << (2 * n) for n, (t, c) in enumerate(row)) for row in STEPS]
+CHUNK_CODE = [sum(c << (2 * n) for n, (t, c) in enumerate(row)) for row in STEPS]
 
 
 def pick(y, table):
@@ -64,9 +64,9 @@
     hidden, down, dec_hidden, gain, freq, place_dev, place_slot, dec_query,
     kw, vw, q_own, q_far, kept,
     part, part_d, rs, rs_d, lat, meta, fresh,
-    qa, qd, m_ref, l_ref, acc, dm, dl, dacc, sbuf, o_far, o_own,
+    qa, qd, m_ref, l_ref, acc, dm, dl, dacc, sbuf, o_own, o_guest,
     ld_sem, q_sems, rs_s, rs_r, rd_s, rd_r, mz_s, mz_r, my_s, my_r,
-    ax_s, ax_r, fz_s, fz_r, nz_s, nz_r, xf_s, xf_r, yf_s, yf_r, yn_s, yn_r, fw_s, fw_r,
+    ax_s, ax_r, fz_s, fz_r, nz_s, nz_r, xf_s, xf_r, yf_s, yf_r, yn_s, yn_r, yo_s, yo_r, zs_s, zs_r,
     sb_s, sb_r, o_sems,
 ):
     seq = lax.axis_index("seq")
@@ -108,7 +108,7 @@
         )
     ]
     loads = [
-        pltpu.make_async_copy(query.at[pl.ds(0, HALF)], q_own, ld_sem.at[0]),
+        pltpu.make_async_copy(query, q_own, ld_sem.at[0]),
         pltpu.make_async_copy(key_w, kw, ld_sem.at[1]),
         pltpu.make_async_copy(cache, kept, ld_sem.at[2]),
         pltpu.make_async_copy(value_w, vw, ld_sem.at[3]),
@@ -156,7 +156,10 @@
     mz = [
         go(remote(mine, mine, mz_s.at[d - 1], mz_r.at[d - 1], at_z(d))) for d in range(1, NZ)
     ]
-    q_copy = go(remote(query.at[pl.ds(HALF, HALF)], q_far, q_sems.at[0], q_sems.at[1], partner))
+    q_copy = remote(
+        query.at[:, pl.ds(GUEST_COL * 192, 768)], q_far, q_sems.at[0], q_sems.at[1], partner
+    )
+    pl.when(y == 3)(lambda: q_copy.start())
 
     m_ref[...] = jnp.full(m_ref.shape, NEG, f32)
     l_ref[...] = jnp.zeros(l_ref.shape, f32)
@@ -168,9 +171,9 @@
         acc[pl.ds(pl.multiple_of(i * 256, 256), 256), :] = jnp.zeros((256, LAT), f32)
         return carry
 
-    lax.fori_loop(0, 2 * SETROWS // 256, clear, 0)
-
-    def absorb(load, dst, base, rows):
+    lax.fori_loop(0, 5 * TQ // 256, clear, 0)
+
+    def absorb(load, dst, base, rows, first=0, last=HEADS // 2):
         def pair(j, carry):
             col = pl.multiple_of(j * 384, 128)
             t0, t1, t2 = load(col), load(col + 128), load(col + 256)
@@ -180,7 +183,7 @@
             ropes = (jnp.where(low, t1, 0.0), jnp.where(low, pltpu.roll(t2, 64, 1), 0.0))
             both = []
             for k in range(2):
-                wcol = pl.multiple_of(j * 256 + k * 128, 128)
+                wcol = pl.multiple_of((first + j) * 256 + k * 128, 128)
                 absorbed = lax.dot_general(
                     nopes[k].astype(bf16), kw[:, pl.ds(wcol, 128)], NT, preferred_element_type=f32
                 )
@@ -189,11 +192,11 @@
             dst[pl.ds(at, 2 * rows), :] = jnp.concatenate(both, 0).astype(bf16)
             return carry
 
-        lax.fori_loop(0, HEADS // 2, pair, 0)
+        lax.fori_loop(0, last - first, pair, 0)
 
     loads[0].wait()
     loads[1].wait()
-    absorb(lambda c: q_own[:, pl.ds(c, 128)].astype(f32), qa, 0, HALF)
+    absorb(lambda c: q_own[:, pl.ds(c, 128)].astype(f32), qa, 0, TOK)
     absorb(
         lambda c: jnp.concatenate(
             [dec_query[0, :, pl.ds(c, 128)], dec_query[1, :, pl.ds(c, 128)]], 0
@@ -232,13 +235,25 @@
         there = lat.at[y, OWN - d, half]
         nz[d] = go(remote(own_half, there, nz_s.at[k], nz_r.at[k], at_z(d)))
 
+    yo = {}
+    for k, d in enumerate((1, -1, 2)):
+        yo[d] = go(remote(own_half, own_half, yo_s.at[k], yo_r.at[k], at_y(d)))
+
+    below, above, across = (y + 3) % NY, (y + 1) % NY, (y + 2) % NY
+
+    def along_z(k, plane_y, d):
+        there = lat.at[plane_y, OWN - d, half]
+        return go(
+            remote(lat.at[plane_y, OWN, half], there, zs_s.at[k], zs_r.at[k], at_z(d))
+        )
+
+    yn = {1: [], -1: []}
+
     def to_planes(i):
         ref = lat.at[y, i, half]
         for w, d in enumerate((1, -1)):
-            yn[d].append(go(remote(ref, ref, yn_s.at[5 * w + i], yn_r.at[5 * w + i], at_y(d))))
-
-    yn = {1: [], -1: []}
-    to_planes(OWN)
+            k = 2 * w + i // 4
+            yn[d].append(go(remote(ref, ref, yn_s.at[k], yn_r.at[k], at_y(d))))
 
     for copy in mz:
         copy.wait_recv()
@@ -269,20 +284,7 @@
     def from_sibling(k, plane_y, start, count):
         to_sibling(k, plane_y, start, count).wait_recv()
 
-    q_copy.wait_recv()
-    absorb(lambda c: q_far[:, pl.ds(c, 128)].astype(f32), qa, SETROWS, HALF)
-
-    for d in (1, -1, 2, -2):
-        nz[d].wait_recv()
-        to_planes(OWN - d)
-    to_sibling(0, y, 0, 5).start()
-    for d in (1, 2, 3):
-        yf[d - 1].wait_recv()
-        xf.append(over_x(d, (y - d + NY) % NY))
-    for copy in xf[0]:
-        copy.wait_recv()
-    to_sibling(1, y, FAR, 3).start()
-
+    ctx = [context[r] for r in range(4)]
     drow = lax.broadcasted_iota(i32, (TOK, 1), 0) % 4
     dstep = lax.broadcasted_iota(i32, (TOK, 1), 0) // 4 % 2
 
@@ -301,24 +303,10 @@
             expo.astype(bf16), contents, dims, preferred_element_type=f32
         )
 
-    for copy in rd_copies:
-        copy.wait_recv()
-    summed = part_d[...]
-    for d in range(1, NHP):
-        summed = summed + rs_d[d - 1]
-    row8 = lax.broadcasted_iota(i32, (8, 1), 0)
-    ctx = [context[r] for r in range(4)]
-    length = pick(row8 % 4, ctx)
-    new_rows = finalize(summed, gain[...], freq[...], (length + row8 // 4).astype(f32))
-    fresh[...] = jnp.concatenate([new_rows.astype(f32), jnp.zeros((TOK - 8, ROW), f32)], 0).astype(
-        bf16
-    )
-    key = lax.broadcasted_iota(i32, (1, TOK), 1)
-    decode_update(
-        lax.dot_general(qd[...], fresh[...], NT, preferred_element_type=f32),
-        (key < 8) & (key % 4 == drow) & (key // 4 <= dstep),
-        fresh[:, :LAT],
-    )
+    @pl.when(y == 0)
+    def _():
+        q_copy.wait_recv()
+        absorb(lambda c: q_far[:, pl.ds(c, 128)].astype(f32), qa, GUEST * TQ, TOK, GUEST_COL // 2)
 
     for copy in my:
         copy.wait_recv()
@@ -339,12 +327,57 @@
     live = (place < pick(hi // 4, ctx)) & (counts < 0.5)
     owner = jnp.where(live, hi // 4, -1)
     loads[2].wait()
-    for r in range(4):
+
+    def kept_rows(r):
         keyrow = jnp.concatenate([owner[4 * r + j : 4 * r + j + 1, :] for j in range(4)], 1)
         scores = jnp.dot(qd[:, :LAT], kept[r, :LAT], preferred_element_type=f32) + jnp.dot(
             qd[:, LAT : LAT + ROPE], kept[r, LAT:], preferred_element_type=f32
         )
         decode_update(scores, keyrow == drow, kept[r, :LAT], NT)
+
+    yo[1].wait_recv()
+    zs_below = [along_z(k, below, d) for k, d in enumerate((1, -1))]
+    yo[-1].wait_recv()
+    zs_above = [along_z(2 + k, above, d) for k, d in enumerate((1, -1))]
+    for d in (1, -1):
+        nz[d].wait_recv()
+    to_sibling(0, y, 1, 3).start()
+    yo[2].wait_recv()
+    zs_across = [along_z(4 + k, across, d) for k, d in enumerate((1, -1, 2, -2))]
+    kept_rows(0)
+    for d in (2, -2):
+        nz[d].wait_recv()
+        to_planes(OWN - d)
+    to_sibling(1, y, 0, 1).start()
+    to_sibling(2, y, 4, 1).start()
+    kept_rows(1)
+    for d in (1, 2, 3):
+        yf[d - 1].wait_recv()
+        xf.append(over_x(d, (y - d + NY) % NY))
+    for copy in xf[0]:
+        copy.wait_recv()
+    to_sibling(3, y, FAR, 3).start()
+    def decode_rest():
+        kept_rows(2)
+        kept_rows(3)
+
+        for copy in rd_copies:
+            copy.wait_recv()
+        summed = part_d[...]
+        for d in range(1, NHP):
+            summed = summed + rs_d[d - 1]
+        row8 = lax.broadcasted_iota(i32, (8, 1), 0)
+        length = pick(row8 % 4, ctx)
+        new_rows = finalize(summed, gain[...], freq[...], (length + row8 // 4).astype(f32))
+        fresh[...] = jnp.concatenate([new_rows.astype(f32), jnp.zeros((TOK - 8, ROW), f32)], 0).astype(
+            bf16
+        )
+        key = lax.broadcasted_iota(i32, (1, TOK), 1)
+        decode_update(
+            lax.dot_general(qd[...], fresh[...], NT, preferred_element_type=f32),
+            (key < 8) & (key % 4 == drow) & (key // 4 <= dstep),
+            fresh[:, :LAT],
+        )
 
     def decode_chunk(c):
         pieces = []
@@ -357,24 +390,27 @@
         )
         decode_update(scores, keyrow == drow, lat[c, :, :, :, :LAT].reshape(CHUNK, LAT))
 
-    set_code, chunk_code = pick(y, SET_CODE), pick(y, CHUNK_CODE)
-
-    def unit(u):
-        return (set_code >> (2 * u)) & 3, (chunk_code >> (2 * u)) & 3
-
-    def rows_of(s, t):
-        return pl.ds(pl.multiple_of(s * SETROWS + t * TQ, TQ), TQ)
-
-    def scores_into(slot, s, c, t):
+    tile_code, chunk_code = pick(y, TILE_CODE), pick(y, CHUNK_CODE)
+
+    def step_of(n):
+        tile = jnp.where((y == 0) & (n >= 4), GUEST, (tile_code >> (2 * n)) & 3)
+        return tile, (chunk_code >> (2 * n)) & 3
+
+    def rows_of(tile):
+        return pl.ds(pl.multiple_of(tile * TQ, TQ), TQ)
+
+    def scores_into(slot, n):
+        tile, c = step_of(n)
         sbuf[slot] = lax.dot_general(
-            qa[rows_of(s, t), :], lat[c].reshape(CHUNK, ROW), NT, preferred_element_type=f32
-        )
-
-    def attend(slot, s, c, t):
-        rows = rows_of(s, t)
-        limit = jnp.where(s == 0, y, NY - 1 - y)
-        start = jnp.where(c == limit, z * TOK + s * HALF, 1 << 20)
-        token = start + lax.broadcasted_iota(i32, (TQ, 1), 0) % HALF
+            qa[rows_of(tile), :], lat[c].reshape(CHUNK, ROW), NT, preferred_element_type=f32
+        )
+
+    def attend(slot, n):
+        tile, c = step_of(n)
+        rows = rows_of(tile)
+        limit = jnp.where(tile == GUEST, 3, y)
+        start = jnp.where(c == limit, z * TOK, 1 << 20)
+        token = start + lax.broadcasted_iota(i32, (TQ, 1), 0) % TOK
         key = (lax.broadcasted_iota(i32, (1, CHUNK), 1) + (z + 6) * TOK) & (CHUNK - 1)
         allowed = key <= token
         scores = jnp.where(allowed, sbuf[slot], NEG)
@@ -391,80 +427,96 @@
             expo.astype(bf16), lat[c, :, :, :, :LAT].reshape(CHUNK, LAT), preferred_element_type=f32
         )
 
-    below, above, across = (y + 3) % NY, (y + 1) % NY, (y + 2) % NY
-
-    def forward(w):
-        ref = lat.at[(below, above)[w], pl.ds(2 * w, 2 + w), half]
-        return remote(ref, ref, fw_s.at[w], fw_r.at[w], at_y(1 - 2 * w))
-
-    def forwarded(w):
-        ref = lat.at[across, pl.ds(2 * w, 2 + w), half]
-        return remote(ref, ref, fw_s.at[w], fw_r.at[w], at_y(1 - 2 * w))
-
-    def near_planes():
-        for w, (d, plane_y) in enumerate(((1, below), (-1, above))):
-            for copy in yn[d]:
+    def near_arrive():
+        for w, (plane_y, spread) in enumerate(((below, zs_below), (above, zs_above))):
+            for copy in spread:
                 copy.wait_recv()
-            forward(w).start()
-            to_sibling(2 + 2 * w, plane_y, 0, 5).start()
-        for w, (dist, plane_y) in enumerate(((1, below), (3, above))):
+            to_sibling(4 + 4 * w, plane_y, 1, 3).start()
+        for w, (d, dist, plane_y) in enumerate(((1, 1, below), (-1, 3, above))):
+            for k, copy in enumerate(yn[d]):
+                copy.wait_recv()
+                to_sibling(5 + 4 * w + k, plane_y, (0, 4)[k], 1).start()
             for copy in xf[dist]:
                 copy.wait_recv()
-            to_sibling(3 + 2 * w, plane_y, FAR, 3).start()
-        for w, plane_y in enumerate((below, above)):
-            from_sibling(2 + 2 * w, plane_y, 0, 5)
-            from_sibling(3 + 2 * w, plane_y, FAR, 3)
-
-    def far_plane():
-        for w in range(2):
-            forwarded(w).wait_recv()
-        for copy in xf[2]:
+            to_sibling(7 + 4 * w, plane_y, FAR, 3).start()
+
+    def near_there(w):
+        plane_y = (below, above)[w]
+        from_sibling(4 + 4 * w, plane_y, 1, 3)
+        from_sibling(5 + 4 * w, plane_y, 0, 1)
+        from_sibling(6 + 4 * w, plane_y, 4, 1)
+        from_sibling(7 + 4 * w, plane_y, FAR, 3)
+
+    def far_arrive():
+        for copy in zs_across + xf[2]:
             copy.wait_recv()
-        to_sibling(6, across, 0, NZ).start()
-        from_sibling(6, across, 0, NZ)
-
-    from_sibling(0, y, 0, 5)
-    from_sibling(1, y, FAR, 3)
-    s0, c0 = unit(0)
-    scores_into(0, s0, c0, 0)
-
-    def one_unit(u, carry):
-        s, c = unit(u)
-        sn, cn = unit(u + 1)
-        scores_into(1, s, c, 1)
-        attend(0, s, c, 0)
-        pl.when(((u == 0) & (y >= 2)) | ((u == 1) & (y < 2)))(near_planes)
-        pl.when(((u == 2) & (y == 2)) | ((u == 3) & (y != 2)))(far_plane)
-        scores_into(0, sn, cn, 0)
-        attend(1, s, c, 1)
-        decode_chunk((y + jnp.where(u == 0, 0, jnp.where(u == 1, 3, u - 1))) % NY)
+        to_sibling(12, across, 0, NZ).start()
+
+    from_sibling(0, y, 1, 3)
+    from_sibling(1, y, 0, 1)
+    from_sibling(2, y, 4, 1)
+    from_sibling(3, y, FAR, 3)
+    scores_into(0, 0)
+    upper = y >= 2
+
+    def near_first():
+        near_arrive()
+        near_there(0)
+
+    def two_steps(i, carry):
+        pl.when((i == 1) & (y == 3))(near_first)
+        scores_into(1, 2 * i + 1)
+        attend(0, 2 * i)
+        pl.when((i == 1) & (y < 3))(near_first)
+        pl.when(i == jnp.where(upper, 2, 1))(lambda: near_there(1))
+        pl.when(i == 2)(far_arrive)
+        pl.when(i == jnp.where(upper, 3, 2))(lambda: from_sibling(12, across, 0, NZ))
+        scores_into(0, 2 * i + 2)
+        attend(1, 2 * i + 1)
+        pl.when(i < 3)(lambda: decode_chunk((y + jnp.where(i == 0, 0, 2 * i + 1)) % NY))
+        pl.when(i == 0)(decode_rest)
         return carry
 
-    lax.fori_loop(0, 4, one_unit, 0)
-    s, c = unit(4)
-    scores_into(1, s, c, 1)
-    attend(0, s, c, 0)
-    attend(1, s, c, 1)
+    pairs = jnp.where(upper, 6, 4)
+    lax.fori_loop(0, pairs - 1, two_steps, 0)
 
     loads[3].wait()
 
-    def project(base, dst):
-        def one(j, carry):
-            for k in range(2):
-                at = pl.ds(pl.multiple_of(base + (2 * j + k) * HALF, HALF), HALF)
-                col = pl.ds(pl.multiple_of((2 * j + k) * VDIM, VDIM), VDIM)
-                total = jnp.sum(l_ref[at, :], -1, keepdims=True)
-                mixed = (acc[at, :] / total).astype(bf16)
-                dst[:, col] = jnp.dot(mixed, vw[:, col], preferred_element_type=f32).astype(bf16)
-            return carry
-
-        lax.fori_loop(0, HEADS // 2, one, 0)
-
-    project(SETROWS, o_far)
-    home = go(remote(o_far, out.at[pl.ds(HALF, HALF)], o_sems.at[0], o_sems.at[1], partner))
-    project(0, o_own)
-    keep = pltpu.make_async_copy(o_own, out.at[pl.ds(0, HALF)], o_sems.at[2])
+    def project(row, h, dst, at):
+        rows = pl.ds(row, TOK)
+        inverse = 1.0 / jnp.sum(l_ref[rows, :], -1, keepdims=True)
+        mixed = (acc[rows, :] * inverse).astype(bf16)
+        dst[:, at * VDIM : (at + 1) * VDIM] = jnp.dot(
+            mixed, vw[:, h * VDIM : (h + 1) * VDIM], preferred_element_type=f32
+        ).astype(bf16)
+
+    home = remote(
+        o_guest, out.at[:, pl.ds(GUEST_COL * VDIM, 512)], o_sems.at[0], o_sems.at[1], partner
+    )
+    scores_into(1, 2 * pairs - 1)
+    attend(0, 2 * pairs - 2)
+    for h in range(8):
+        project(h * TOK, h, o_own, h)
+    attend(1, 2 * pairs - 1)
+    decode_chunk(across)
+
+    @pl.when(y == 0)
+    def _():
+        for h in range(GUEST_COL, HEADS):
+            project((h + 4) * TOK, h, o_guest, h - GUEST_COL)
+        home.start()
+
+    for h in range(8, HEADS):
+        project(h * TOK, h, o_own, h)
+    keep = pltpu.make_async_copy(
+        o_own.at[:, pl.ds(0, GUEST_COL * VDIM)], out.at[:, pl.ds(0, GUEST_COL * VDIM)], o_sems.at[2]
+    )
     keep.start()
+    keep_rest = pltpu.make_async_copy(
+        o_own.at[:, pl.ds(GUEST_COL * VDIM, 512)], out.at[:, pl.ds(GUEST_COL * VDIM, 512)],
+        o_sems.at[3],
+    )
+    pl.when(y < 3)(lambda: keep_rest.start())
     dmixed = dacc[...] / jnp.sum(dl[...], -1, keepdims=True)
     for h in range(HEADS):
         col = slice(h * VDIM, (h + 1) * VDIM)
@@ -476,15 +528,27 @@
 
     for copy in sends:
         copy.wait_send()
-    for w in range(2):
-        forward(w).wait_send()
-        to_sibling(2 + 2 * w, (below, above)[w], 0, 5).wait_send()
-        to_sibling(3 + 2 * w, (below, above)[w], FAR, 3).wait_send()
-    to_sibling(0, y, 0, 5).wait_send()
-    to_sibling(1, y, FAR, 3).wait_send()
-    to_sibling(6, across, 0, NZ).wait_send()
+    for w, plane_y in enumerate((below, above)):
+        to_sibling(4 + 4 * w, plane_y, 1, 3).wait_send()
+        to_sibling(5 + 4 * w, plane_y, 0, 1).wait_send()
+        to_sibling(6 + 4 * w, plane_y, 4, 1).wait_send()
+        to_sibling(7 + 4 * w, plane_y, FAR, 3).wait_send()
+    to_sibling(0, y, 1, 3).wait_send()
+    to_sibling(1, y, 0, 1).wait_send()
+    to_sibling(2, y, 4, 1).wait_send()
+    to_sibling(3, y, FAR, 3).wait_send()
+    to_sibling(12, across, 0, NZ).wait_send()
     keep.wait()
-    home.wait_recv()
+    pl.when(y < 3)(lambda: keep_rest.wait())
+
+    @pl.when(y == 0)
+    def _():
+        home.wait_send()
+
+    @pl.when(y == 3)
+    def _():
+        q_copy.wait_send()
+        home.wait_recv()
 
 
 def on_device(
@@ -516,8 +580,8 @@
             pltpu.VMEM((2, 4, HEADS * 192), bf16),
             pltpu.VMEM((LAT, HEADS * NOPE), bf16),
             pltpu.VMEM((LAT, HEADS * VDIM), bf16),
-            pltpu.VMEM((HALF, HEADS * 192), bf16),
-            pltpu.VMEM((HALF, HEADS * 192), bf16),
+            pltpu.VMEM((TOK, HEADS * 192), bf16),
+            pltpu.VMEM((TOK, 4 * 192), bf16),
             pltpu.VMEM((4, LAT + ROPE, 512), bf16),
             pltpu.VMEM((TOK, ROW), f32),
             pltpu.VMEM((8, ROW), f32),
@@ -526,22 +590,22 @@
             pltpu.VMEM((NY, NZ, NHP, 16, ROW), bf16),
             pltpu.VMEM((NY * NZ, 8, TOK), i32),
             pltpu.VMEM((TOK, ROW), bf16),
-            pltpu.VMEM((2 * SETROWS, ROW), bf16),
+            pltpu.VMEM((5 * TQ, ROW), bf16),
             pltpu.VMEM((TOK, ROW), bf16),
-            pltpu.VMEM((2 * SETROWS, 128), f32),
-            pltpu.VMEM((2 * SETROWS, 128), f32),
-            pltpu.VMEM((2 * SETROWS, LAT), f32),
+            pltpu.VMEM((5 * TQ, 128), f32),
+            pltpu.VMEM((5 * TQ, 128), f32),
+            pltpu.VMEM((5 * TQ, LAT), f32),
             pltpu.VMEM((TOK, 128), f32),
             pltpu.VMEM((TOK, 128), f32),
             pltpu.VMEM((TOK, LAT), f32),
             pltpu.VMEM((2, TQ, CHUNK), f32),
-            pltpu.VMEM((HALF, HEADS * VDIM), bf16),
-            pltpu.VMEM((HALF, HEADS * VDIM), bf16),
+            pltpu.VMEM((TOK, HEADS * VDIM), bf16),
+            pltpu.VMEM((TOK, 4 * VDIM), bf16),
             dma((12,)), dma((2,)), dma((7,)), dma((7,)), dma((7,)), dma((7,)),
             dma((7,)), dma((7,)), dma((3,)), dma((3,)),
             dma((3,)), dma((3,)), dma((3,)), dma((3,)), dma((4,)), dma((4,)),
-            dma((12,)), dma((12,)), dma((3,)), dma((3,)), dma((10,)), dma((10,)),
-            dma((2,)), dma((2,)), dma((7,)), dma((7,)), dma((3,)),
+            dma((12,)), dma((12,)), dma((3,)), dma((3,)), dma((4,)), dma((4,)),
+            dma((3,)), dma((3,)), dma((8,)), dma((8,)), dma((13,)), dma((13,)), dma((4,)),
         ],
         compiler_params=pltpu.CompilerParams(
             collective_id=0, has_side_effects=True, vmem_limit_bytes=56 << 20

time: 74.3 us -> 68.3 us (0.919)
  Pallas kernels: 70.1 us -> 63.8 us
    pallas_call x1, Pallas kernels: 70.1 us -> 63.8 us  [on_device(): pl.pallas_call(kernel, out_shape=(jax.ShapeDtypeStruct((TOK, HEADS * VDIM...]
where the time goes in v3:
time: 68.3 us; the launch traced here: 67.7 us
  Pallas kernels  63.8 us (93%)
  local copies, waits for them, and re-layouts  3.27 us (5%)
    pallas_call x1, Pallas kernels, on_device(): pl.pallas_call(kernel, out_shape=(jax.ShapeDtypeStruct((TOK, HEADS * VDIM...  63.8 us
    unnamed x2, local copies, waits for them, and re-layouts  3.27 us

profile of v3, /device:TPU:24, one launch (start us, length us, event | category | flops | bytes accessed | tf_op | source)
XLA Modules:
  0.0 67.7 jit_solution(2630495526611366273)
XLA Ops:
  0.6 63.8 %shard_map.140 = (bf16[128,2048]{1,0:T(8,128)(2,1)}, bf16[2,4,2048]{2,1,0:T(4,128)(2,1)}) custom-call(bf16[128,896]{1,0:T(8,128)(2,1)} %hidden_in.1, bf16[576,896]{1,0:T(8,128)(2,1)} %bitcast.6, bf16[2,4,896]{2,1,0:T(4,128)(2,1)} %dec_hidden_in.1, f32[1,512]{1,0:T(1,128)} %bitcast.7, f32[1,128]{1,0:T(1,128)} %constant.2.clone.freq_in, s32[1,128]{1,0:T(1,128)} %bitcast.8, ...), custom_call_target="tpu_custom_call" | custom-call | tf_op jit(solution)/shard_map/pallas_call | solution.py:564
  64.4 1.9 %copy.17 = bf16[128,2048]{1,0:T(8,128)(2,1)} copy(bf16[128,2048]{1,0:T(8,128)(2,1)} %get-tuple-element.4) | data formatting | bytes 1048576
  66.3 1.4 %copy.18 = bf16[2,4,2048]{2,1,0:T(4,128)(2,1)} copy(bf16[2,4,2048]{2,1,0:T(4,128)(2,1)} %get-tuple-element.5) | data formatting | bytes 65536

commit v4 on v3

--- a/solution.py
+++ b/solution.py
@@ -21,7 +21,6 @@
 OWN, FAR = 2, 5
 TQ = 512
 GUEST = 4
-GUEST_COL = 12
 SCALE = (NOPE + ROPE) ** (-0.5) * 1.4426950408889634
 NEG = -1e30
 MESH = pl.DeviceIdType.MESH
@@ -32,7 +31,7 @@
     [(0, 0), (1, 0), (2, 0), (3, 0), (0, 0), (0, 1), (0, 3), (0, 2)],
     [(t, c) for c in (1, 0) for t in range(4)],
     [(t, c) for c in (2, 1, 0) for t in range(4)],
-    [(t, c) for c in (3, 2, 0, 1) for t in range(3)],
+    [(t, c) for c in (3, 2, 0, 1) for t in (1, 2, 3)],
 ]
 TILE_CODE = [sum(t << (2 * n) for n, (t, c) in enumerate(row)) for row in STEPS]
 CHUNK_CODE = [sum(c << (2 * n) for n, (t, c) in enumerate(row)) for row in STEPS]
@@ -64,7 +63,7 @@
     hidden, down, dec_hidden, gain, freq, place_dev, place_slot, dec_query,
     kw, vw, q_own, q_far, kept,
     part, part_d, rs, rs_d, lat, meta, fresh,
-    qa, qd, m_ref, l_ref, acc, dm, dl, dacc, sbuf, o_own, o_guest,
+    qa, qd, m_ref, l_ref, acc, dm, dl, dacc, ks, sbuf, o_own, o_guest,
     ld_sem, q_sems, rs_s, rs_r, rd_s, rd_r, mz_s, mz_r, my_s, my_r,
     ax_s, ax_r, fz_s, fz_r, nz_s, nz_r, xf_s, xf_r, yf_s, yf_r, yn_s, yn_r, yo_s, yo_r, zs_s, zs_r,
     sb_s, sb_r, o_sems,
@@ -157,7 +156,7 @@
         go(remote(mine, mine, mz_s.at[d - 1], mz_r.at[d - 1], at_z(d))) for d in range(1, NZ)
     ]
     q_copy = remote(
-        query.at[:, pl.ds(GUEST_COL * 192, 768)], q_far, q_sems.at[0], q_sems.at[1], partner
+        query.at[:, pl.ds(0, 768)], q_far, q_sems.at[0], q_sems.at[1], partner
     )
     pl.when(y == 3)(lambda: q_copy.start())
 
@@ -173,7 +172,7 @@
 
     lax.fori_loop(0, 5 * TQ // 256, clear, 0)
 
-    def absorb(load, dst, base, rows, first=0, last=HEADS // 2):
+    def absorb(load, dst, base, rows, heads=HEADS):
         def pair(j, carry):
             col = pl.multiple_of(j * 384, 128)
             t0, t1, t2 = load(col), load(col + 128), load(col + 256)
@@ -183,7 +182,7 @@
             ropes = (jnp.where(low, t1, 0.0), jnp.where(low, pltpu.roll(t2, 64, 1), 0.0))
             both = []
             for k in range(2):
-                wcol = pl.multiple_of((first + j) * 256 + k * 128, 128)
+                wcol = pl.multiple_of(j * 256 + k * 128, 128)
                 absorbed = lax.dot_general(
                     nopes[k].astype(bf16), kw[:, pl.ds(wcol, 128)], NT, preferred_element_type=f32
                 )
@@ -192,7 +191,7 @@
             dst[pl.ds(at, 2 * rows), :] = jnp.concatenate(both, 0).astype(bf16)
             return carry
 
-        lax.fori_loop(0, last - first, pair, 0)
+        lax.fori_loop(0, heads // 2, pair, 0)
 
     loads[0].wait()
     loads[1].wait()
@@ -203,6 +202,12 @@
         ).astype(f32),
         qd, 0, 8,
     )
+
+    loads[2].wait()
+    for r in range(4):
+        ks[:, 512 * r : 512 * (r + 1)] = jnp.dot(
+            qd[:, :LAT], kept[r, :LAT], preferred_element_type=f32
+        ) + jnp.dot(qd[:, LAT : LAT + ROPE], kept[r, LAT:], preferred_element_type=f32)
 
     for copy in rs_copies:
         copy.wait_recv()
@@ -273,7 +278,7 @@
 
     for copy in fz:
         copy.wait_recv()
-    xf = [over_x(0, y)]
+    xf = {0: over_x(0, y)}
     far_rows = lat.at[y, pl.ds(FAR, 3), hp]
     yf = [go(remote(far_rows, far_rows, yf_s.at[d - 1], yf_r.at[d - 1], at_y(d))) for d in (1, 2, 3)]
 
@@ -288,7 +293,7 @@
     drow = lax.broadcasted_iota(i32, (TOK, 1), 0) % 4
     dstep = lax.broadcasted_iota(i32, (TOK, 1), 0) // 4 % 2
 
-    def decode_update(scores, mask, contents, dims=(((1,), (0,)), ((), ()))):
+    def decode_weights(scores, mask):
         scores = jnp.where(mask, scores * SCALE, NEG)
         m_old = dm[...]
         m_new = jnp.maximum(m_old, jnp.max(scores, -1, keepdims=True))
@@ -299,15 +304,44 @@
         for j in range(scores.shape[1] // 128):
             total = total + expo[:, 128 * j : 128 * (j + 1)]
         dl[...] = total
-        dacc[...] = dacc[...] * alpha[:, :1] + lax.dot_general(
-            expo.astype(bf16), contents, dims, preferred_element_type=f32
-        )
+        dacc[...] = dacc[...] * alpha[:, :1]
+        return expo.astype(bf16)
+
+    def decode_update(scores, mask, contents):
+        expo = decode_weights(scores, mask)
+        dacc[...] = dacc[...] + jnp.dot(expo, contents, preferred_element_type=f32)
 
     @pl.when(y == 0)
     def _():
         q_copy.wait_recv()
-        absorb(lambda c: q_far[:, pl.ds(c, 128)].astype(f32), qa, GUEST * TQ, TOK, GUEST_COL // 2)
-
+        absorb(lambda c: q_far[:, pl.ds(c, 128)].astype(f32), qa, GUEST * TQ, TOK, 4)
+
+    yo[1].wait_recv()
+    zs_below = [along_z(k, below, d) for k, d in enumerate((1, -1))]
+    yo[-1].wait_recv()
+    zs_above = [along_z(2 + k, above, d) for k, d in enumerate((1, -1))]
+    for copy in rd_copies:
+        copy.wait_recv()
+    summed = part_d[...]
+    for d in range(1, NHP):
+        summed = summed + rs_d[d - 1]
+    row8 = lax.broadcasted_iota(i32, (8, 1), 0)
+    length = pick(row8 % 4, ctx)
+    new_rows = finalize(summed, gain[...], freq[...], (length + row8 // 4).astype(f32))
+    fresh[...] = jnp.concatenate([new_rows.astype(f32), jnp.zeros((TOK - 8, ROW), f32)], 0).astype(
+        bf16
+    )
+    key = lax.broadcasted_iota(i32, (1, TOK), 1)
+    decode_update(
+        lax.dot_general(qd[...], fresh[...], NT, preferred_element_type=f32),
+        (key < 8) & (key % 4 == drow) & (key // 4 <= dstep),
+        fresh[:, :LAT],
+    )
+    for d in (1, -1):
+        nz[d].wait_recv()
+    to_sibling(0, y, 1, 3).start()
+    yo[2].wait_recv()
+    zs_across = [along_z(4 + k, across, d) for k, d in enumerate((1, -1, 2, -2))]
     for copy in my:
         copy.wait_recv()
     counts = jnp.zeros((16, TOK), f32)
@@ -326,58 +360,30 @@
     place = hi % 4 * 128 + lax.broadcasted_iota(i32, (16, TOK), 1)
     live = (place < pick(hi // 4, ctx)) & (counts < 0.5)
     owner = jnp.where(live, hi // 4, -1)
-    loads[2].wait()
-
-    def kept_rows(r):
-        keyrow = jnp.concatenate([owner[4 * r + j : 4 * r + j + 1, :] for j in range(4)], 1)
-        scores = jnp.dot(qd[:, :LAT], kept[r, :LAT], preferred_element_type=f32) + jnp.dot(
-            qd[:, LAT : LAT + ROPE], kept[r, LAT:], preferred_element_type=f32
-        )
-        decode_update(scores, keyrow == drow, kept[r, :LAT], NT)
-
-    yo[1].wait_recv()
-    zs_below = [along_z(k, below, d) for k, d in enumerate((1, -1))]
-    yo[-1].wait_recv()
-    zs_above = [along_z(2 + k, above, d) for k, d in enumerate((1, -1))]
-    for d in (1, -1):
-        nz[d].wait_recv()
-    to_sibling(0, y, 1, 3).start()
-    yo[2].wait_recv()
-    zs_across = [along_z(4 + k, across, d) for k, d in enumerate((1, -1, 2, -2))]
-    kept_rows(0)
+
+    def kept_rows():
+        keyrow = jnp.concatenate([owner[j : j + 1, :] for j in range(16)], 1)
+        expo = decode_weights(ks[...], keyrow == drow)
+        mixed = dacc[...]
+        for r in range(4):
+            mixed = mixed + lax.dot_general(
+                expo[:, 512 * r : 512 * (r + 1)], kept[r, :LAT], NT, preferred_element_type=f32
+            )
+        dacc[...] = mixed
+
     for d in (2, -2):
         nz[d].wait_recv()
         to_planes(OWN - d)
     to_sibling(1, y, 0, 1).start()
     to_sibling(2, y, 4, 1).start()
-    kept_rows(1)
-    for d in (1, 2, 3):
-        yf[d - 1].wait_recv()
-        xf.append(over_x(d, (y - d + NY) % NY))
     for copy in xf[0]:
         copy.wait_recv()
     to_sibling(3, y, FAR, 3).start()
-    def decode_rest():
-        kept_rows(2)
-        kept_rows(3)
-
-        for copy in rd_copies:
-            copy.wait_recv()
-        summed = part_d[...]
-        for d in range(1, NHP):
-            summed = summed + rs_d[d - 1]
-        row8 = lax.broadcasted_iota(i32, (8, 1), 0)
-        length = pick(row8 % 4, ctx)
-        new_rows = finalize(summed, gain[...], freq[...], (length + row8 // 4).astype(f32))
-        fresh[...] = jnp.concatenate([new_rows.astype(f32), jnp.zeros((TOK - 8, ROW), f32)], 0).astype(
-            bf16
-        )
-        key = lax.broadcasted_iota(i32, (1, TOK), 1)
-        decode_update(
-            lax.dot_general(qd[...], fresh[...], NT, preferred_element_type=f32),
-            (key < 8) & (key % 4 == drow) & (key // 4 <= dstep),
-            fresh[:, :LAT],
-        )
+    for d in (1, 3, 2):
+        yf[d - 1].wait_recv()
+        xf[d] = over_x(d, (y - d + NY) % NY)
+
+    kept_rows()
 
     def decode_chunk(c):
         pieces = []
@@ -474,7 +480,7 @@
         scores_into(0, 2 * i + 2)
         attend(1, 2 * i + 1)
         pl.when(i < 3)(lambda: decode_chunk((y + jnp.where(i == 0, 0, 2 * i + 1)) % NY))
-        pl.when(i == 0)(decode_rest)
+        pl.when(i == jnp.where(upper, 3, 2))(lambda: decode_chunk(across))
         return carry
 
     pairs = jnp.where(upper, 6, 4)
@@ -482,50 +488,48 @@
 
     loads[3].wait()
 
-    def project(row, h, dst, at):
+    dmixed = dacc[...] * (1.0 / jnp.sum(dl[...], -1, keepdims=True))
+
+    def mixed_of(row):
         rows = pl.ds(row, TOK)
-        inverse = 1.0 / jnp.sum(l_ref[rows, :], -1, keepdims=True)
-        mixed = (acc[rows, :] * inverse).astype(bf16)
-        dst[:, at * VDIM : (at + 1) * VDIM] = jnp.dot(
-            mixed, vw[:, h * VDIM : (h + 1) * VDIM], preferred_element_type=f32
-        ).astype(bf16)
-
-    home = remote(
-        o_guest, out.at[:, pl.ds(GUEST_COL * VDIM, 512)], o_sems.at[0], o_sems.at[1], partner
-    )
+        return acc[rows, :] * (1.0 / jnp.sum(l_ref[rows, :], -1, keepdims=True))
+
+    def through(mixed, h):
+        weight = vw[:, h * VDIM : (h + 1) * VDIM]
+        return jnp.dot(mixed.astype(bf16), weight, preferred_element_type=f32).astype(bf16)
+
+    def project(h):
+        both = jnp.concatenate([mixed_of(h * TOK), dmixed[8 * h : 8 * h + 8]], 0)
+        res = through(both, h)
+        col = slice(h * VDIM, (h + 1) * VDIM)
+        o_own[:, col] = res[:TOK]
+        dec_out[0, :, col] = res[TOK : TOK + 4]
+        dec_out[1, :, col] = res[TOK + 4 :]
+
+    home = remote(o_guest, out.at[:, pl.ds(0, 512)], o_sems.at[0], o_sems.at[1], partner)
+
+    def keep(k):
+        cols = pl.ds(512 * k, 512)
+        return pltpu.make_async_copy(o_own.at[:, cols], out.at[:, cols], o_sems.at[2 + k])
+
     scores_into(1, 2 * pairs - 1)
     attend(0, 2 * pairs - 2)
-    for h in range(8):
-        project(h * TOK, h, o_own, h)
+    for h in range(12):
+        project(h)
     attend(1, 2 * pairs - 1)
-    decode_chunk(across)
+    pl.when(y < 3)(lambda: keep(0).start())
+    keep(1).start()
+    keep(2).start()
 
     @pl.when(y == 0)
     def _():
-        for h in range(GUEST_COL, HEADS):
-            project((h + 4) * TOK, h, o_guest, h - GUEST_COL)
+        for h in range(4):
+            o_guest[:, h * VDIM : (h + 1) * VDIM] = through(mixed_of(GUEST * TQ + h * TOK), h)
         home.start()
 
-    for h in range(8, HEADS):
-        project(h * TOK, h, o_own, h)
-    keep = pltpu.make_async_copy(
-        o_own.at[:, pl.ds(0, GUEST_COL * VDIM)], out.at[:, pl.ds(0, GUEST_COL * VDIM)], o_sems.at[2]
-    )
-    keep.start()
-    keep_rest = pltpu.make_async_copy(
-        o_own.at[:, pl.ds(GUEST_COL * VDIM, 512)], out.at[:, pl.ds(GUEST_COL * VDIM, 512)],
-        o_sems.at[3],
-    )
-    pl.when(y < 3)(lambda: keep_rest.start())
-    dmixed = dacc[...] / jnp.sum(dl[...], -1, keepdims=True)
-    for h in range(HEADS):
-        col = slice(h * VDIM, (h + 1) * VDIM)
-        res = jnp.dot(
-            dmixed[8 * h : 8 * h + 8].astype(bf16), vw[:, col], preferred_element_type=f32
-        ).astype(bf16)
-        dec_out[0, :, col] = res[0:4]
-        dec_out[1, :, col] = res[4:8]
-
+    for h in range(12, HEADS):
+        project(h)
+    keep(3).start()
     for copy in sends:
         copy.wait_send()
     for w, plane_y in enumerate((below, above)):
@@ -538,8 +542,9 @@
     to_sibling(2, y, 4, 1).wait_send()
     to_sibling(3, y, FAR, 3).wait_send()
     to_sibling(12, across, 0, NZ).wait_send()
-    keep.wait()
-    pl.when(y < 3)(lambda: keep_rest.wait())
+    pl.when(y < 3)(lambda: keep(0).wait())
+    for k in (1, 2, 3):
+        keep(k).wait()
 
     @pl.when(y == 0)
     def _():
@@ -549,6 +554,11 @@
     def _():
         q_copy.wait_send()
         home.wait_recv()
+
+
+def hand_over(a, b, a_out, b_out):
+    a_out[...] = a[...]
+    b_out[...] = b[...]
 
 
 def on_device(
@@ -561,7 +571,7 @@
     vmem = pl.BlockSpec(memory_space=pltpu.VMEM)
     hbm = pl.BlockSpec(memory_space=pl.ANY)
     dma = pltpu.SemaphoreType.DMA
-    return pl.pallas_call(
+    out, dec_out = pl.pallas_call(
         kernel,
         out_shape=(
             jax.ShapeDtypeStruct((TOK, HEADS * VDIM), bf16),
@@ -598,6 +608,7 @@
             pltpu.VMEM((TOK, 128), f32),
             pltpu.VMEM((TOK, 128), f32),
             pltpu.VMEM((TOK, LAT), f32),
+            pltpu.VMEM((TOK, 2048), f32),
             pltpu.VMEM((2, TQ, CHUNK), f32),
             pltpu.VMEM((TOK, HEADS * VDIM), bf16),
             pltpu.VMEM((TOK, 4 * VDIM), bf16),
@@ -605,7 +616,7 @@
             dma((7,)), dma((7,)), dma((3,)), dma((3,)),
             dma((3,)), dma((3,)), dma((3,)), dma((3,)), dma((4,)), dma((4,)),
             dma((12,)), dma((12,)), dma((3,)), dma((3,)), dma((4,)), dma((4,)),
-            dma((3,)), dma((3,)), dma((8,)), dma((8,)), dma((13,)), dma((13,)), dma((4,)),
+            dma((3,)), dma((3,)), dma((8,)), dma((8,)), dma((13,)), dma((13,)), dma((6,)),
         ],
         compiler_params=pltpu.CompilerParams(
             collective_id=0, has_side_effects=True, vmem_limit_bytes=56 << 20
@@ -615,6 +626,15 @@
         place_device.reshape(1, TOK), place_slot.reshape(1, TOK), decode_query, context_length,
         key_weight, value_weight, prefill_query, latent_cache.transpose(0, 2, 1),
     )
+    return pl.pallas_call(
+        hand_over,
+        out_shape=(
+            jax.ShapeDtypeStruct((TOK, HEADS * VDIM), bf16),
+            jax.ShapeDtypeStruct((2, 4, HEADS * VDIM), bf16),
+        ),
+        in_specs=[vmem, vmem],
+        out_specs=(vmem, vmem),
+    )(out, dec_out)
 
 
 def solution(mesh):

time: 68.3 us -> 64.6 us (0.946)
  local copies, waits for them, and re-layouts: 3.27 us -> 0 us
  Pallas kernels: 63.8 us -> 63 us
    unnamed x2 -> x0, local copies, waits for them, and re-layouts: 3.27 us -> none
    pallas_call x1, Pallas kernels: 63.8 us -> 61.1 us  [on_device(): pl.pallas_call(kernel, out_shape=(jax.ShapeDtypeStruct((TOK, HEADS * VDIM...]
    pallas_call x0 -> x1, Pallas kernels: none -> 1.87 us  [on_device(): pl.pallas_call(hand_over, out_shape=(jax.ShapeDtypeStruct((TOK, HEADS * V...]
where the time goes in v4:
time: 64.6 us; the launch traced here: 63.6 us
  Pallas kernels  63 us (98%)
    pallas_call x1, Pallas kernels, on_device(): pl.pallas_call(kernel, out_shape=(jax.ShapeDtypeStruct((TOK, HEADS * VDIM...  61.1 us
    pallas_call x1, Pallas kernels, on_device(): pl.pallas_call(hand_over, out_shape=(jax.ShapeDtypeStruct((TOK, HEADS * V...  1.87 us

profile of v4, /device:TPU:24, one launch (start us, length us, event | category | flops | bytes accessed | tf_op | source)
XLA Modules:
  0.0 63.6 jit_solution(10645755296782913023)
XLA Ops:
  0.6 61.1 %shard_map.140 = (bf16[128,2048]{1,0:T(8,128)(2,1)}, bf16[2,4,2048]{2,1,0:T(4,128)(2,1)}) custom-call(bf16[128,896]{1,0:T(8,128)(2,1)} %hidden_in.1, bf16[576,896]{1,0:T(8,128)(2,1)} %bitcast.6, bf16[2,4,896]{2,1,0:T(4,128)(2,1)} %dec_hidden_in.1, f32[1,512]{1,0:T(1,128)} %bitcast.7, f32[1,128]{1,0:T(1,128)} %constant.2.clone.freq_in, s32[1,128]{1,0:T(1,128)} %bitcast.8, ...), custom_call_target="tpu_custom_call" | custom-call | tf_op jit(solution)/shard_map/pallas_call | solution.py:574
  61.8 1.9 %shard_map.141 = (bf16[128,2048]{1,0:T(8,128)(2,1)}, bf16[2,4,2048]{2,1,0:T(4,128)(2,1)}) custom-call(bf16[128,2048]{1,0:T(8,128)(2,1)} %get-tuple-element.4.a, bf16[2,4,2048]{2,1,0:T(4,128)(2,1)} %get-tuple-element.5.b), custom_call_target="tpu_custom_call" | custom-call | tf_op jit(solution)/shard_map/pallas_call | solution.py:629

commit v5 on v4

--- a/solution.py
+++ b/solution.py
@@ -385,16 +385,25 @@
 
     kept_rows()
 
-    def decode_chunk(c):
-        pieces = []
-        for j in range(NZ):
-            tile = meta[pl.ds(c * NZ + (z + j + 6) % NZ, 1), :, :][0]
-            pieces.append(jnp.where(tile[0:1] == seq, tile[1:2] // 512, -1))
-        keyrow = jnp.concatenate(pieces, 1)
-        scores = lax.dot_general(
-            qd[...], lat[c].reshape(CHUNK, ROW), NT, preferred_element_type=f32
-        )
-        decode_update(scores, keyrow == drow, lat[c, :, :, :, :LAT].reshape(CHUNK, LAT))
+    def decode_chunks(*planes):
+        pieces, scores = [], []
+        for c in planes:
+            for j in range(NZ):
+                tile = meta[pl.ds(c * NZ + (z + j + 6) % NZ, 1), :, :][0]
+                pieces.append(jnp.where(tile[0:1] == seq, tile[1:2] // 512, -1))
+            scores.append(
+                lax.dot_general(
+                    qd[...], lat[c].reshape(CHUNK, ROW), NT, preferred_element_type=f32
+                )
+            )
+        expo = decode_weights(jnp.concatenate(scores, 1), jnp.concatenate(pieces, 1) == drow)
+        mixed = dacc[...]
+        for k, c in enumerate(planes):
+            mixed = mixed + jnp.dot(
+                expo[:, CHUNK * k : CHUNK * (k + 1)], lat[c, :, :, :, :LAT].reshape(CHUNK, LAT),
+                preferred_element_type=f32,
+            )
+        dacc[...] = mixed
 
     tile_code, chunk_code = pick(y, TILE_CODE), pick(y, CHUNK_CODE)
 
@@ -479,8 +488,7 @@
         pl.when(i == jnp.where(upper, 3, 2))(lambda: from_sibling(12, across, 0, NZ))
         scores_into(0, 2 * i + 2)
         attend(1, 2 * i + 1)
-        pl.when(i < 3)(lambda: decode_chunk((y + jnp.where(i == 0, 0, 2 * i + 1)) % NY))
-        pl.when(i == jnp.where(upper, 3, 2))(lambda: decode_chunk(across))
+        pl.when(i == jnp.where(upper, 3, 2))(lambda: decode_chunks(y, below, above, across))
         return carry
 
     pairs = jnp.where(upper, 6, 4)

time: 64.6 us -> 63.5 us (0.983)
  Pallas kernels: 63 us -> 61.9 us
    pallas_call x1, Pallas kernels: 61.1 us -> 60 us  [on_device(): pl.pallas_call(kernel, out_shape=(jax.ShapeDtypeStruct((TOK, HEADS * VDIM...]
where the time goes in v5:
time: 63.5 us; the launch traced here: 62.5 us
  Pallas kernels  61.9 us (97%)
  between operations  0.64 us (1%)
    pallas_call x1, Pallas kernels, on_device(): pl.pallas_call(kernel, out_shape=(jax.ShapeDtypeStruct((TOK, HEADS * VDIM...  60 us
    pallas_call x1, Pallas kernels, on_device(): pl.pallas_call(hand_over, out_shape=(jax.ShapeDtypeStruct((TOK, HEADS * V...  1.87 us

profile of v5, /device:TPU:24, one launch (start us, length us, event | category | flops | bytes accessed | tf_op | source)
XLA Modules:
  0.0 62.5 jit_solution(13121182765534709527)
XLA Ops:
  0.6 60.0 %shard_map.140 = (bf16[128,2048]{1,0:T(8,128)(2,1)}, bf16[2,4,2048]{2,1,0:T(4,128)(2,1)}) custom-call(bf16[128,896]{1,0:T(8,128)(2,1)} %hidden_in.1, bf16[576,896]{1,0:T(8,128)(2,1)} %bitcast.6, bf16[2,4,896]{2,1,0:T(4,128)(2,1)} %dec_hidden_in.1, f32[1,512]{1,0:T(1,128)} %bitcast.7, f32[1,128]{1,0:T(1,128)} %constant.2.clone.freq_in, s32[1,128]{1,0:T(1,128)} %bitcast.8, ...), custom_call_target="tpu_custom_call" | custom-call | tf_op jit(solution)/shard_map/pallas_call | solution.py:582
  60.6 1.9 %shard_map.141 = (bf16[128,2048]{1,0:T(8,128)(2,1)}, bf16[2,4,2048]{2,1,0:T(4,128)(2,1)}) custom-call(bf16[128,2048]{1,0:T(8,128)(2,1)} %get-tuple-element.4.a, bf16[2,4,2048]{2,1,0:T(4,128)(2,1)} %get-tuple-element.5.b), custom_call_target="tpu_custom_call" | custom-call | tf_op jit(solution)/shard_map/pallas_call | solution.py:637

commit v6 on v5

--- a/solution.py
+++ b/solution.py
@@ -488,13 +488,15 @@
         pl.when(i == jnp.where(upper, 3, 2))(lambda: from_sibling(12, across, 0, NZ))
         scores_into(0, 2 * i + 2)
         attend(1, 2 * i + 1)
-        pl.when(i == jnp.where(upper, 3, 2))(lambda: decode_chunks(y, below, above, across))
         return carry
 
     pairs = jnp.where(upper, 6, 4)
     lax.fori_loop(0, pairs - 1, two_steps, 0)
 
     loads[3].wait()
+    scores_into(1, 2 * pairs - 1)
+    attend(0, 2 * pairs - 2)
+    decode_chunks(y, below, above, across)
 
     dmixed = dacc[...] * (1.0 / jnp.sum(dl[...], -1, keepdims=True))
 
@@ -520,8 +522,6 @@
         cols = pl.ds(512 * k, 512)
         return pltpu.make_async_copy(o_own.at[:, cols], out.at[:, cols], o_sems.at[2 + k])
 
-    scores_into(1, 2 * pairs - 1)
-    attend(0, 2 * pairs - 2)
     for h in range(12):
         project(h)
     attend(1, 2 * pairs - 1)

time: 63.5 us -> 63.2 us (level)
  no operation moved by 1% of the time
where the time goes in v6:
time: 63.2 us; the launch traced here: 62.2 us
  Pallas kernels  61.5 us (97%)
  between operations  0.64 us (1%)
    pallas_call x1, Pallas kernels, on_device(): pl.pallas_call(kernel, out_shape=(jax.ShapeDtypeStruct((TOK, HEADS * VDIM...  59.7 us
    pallas_call x1, Pallas kernels, on_device(): pl.pallas_call(hand_over, out_shape=(jax.ShapeDtypeStruct((TOK, HEADS * V...  1.87 us

profile of v6, /device:TPU:24, one launch (start us, length us, event | category | flops | bytes accessed | tf_op | source)
XLA Modules:
  0.0 62.2 jit_solution(10740560223103335188)
XLA Ops:
  0.6 59.7 %shard_map.140 = (bf16[128,2048]{1,0:T(8,128)(2,1)}, bf16[2,4,2048]{2,1,0:T(4,128)(2,1)}) custom-call(bf16[128,896]{1,0:T(8,128)(2,1)} %hidden_in.1, bf16[576,896]{1,0:T(8,128)(2,1)} %bitcast.6, bf16[2,4,896]{2,1,0:T(4,128)(2,1)} %dec_hidden_in.1, f32[1,512]{1,0:T(1,128)} %bitcast.7, f32[1,128]{1,0:T(1,128)} %constant.2.clone.freq_in, s32[1,128]{1,0:T(1,128)} %bitcast.8, ...), custom_call_target="tpu_custom_call" | custom-call | tf_op jit(solution)/shard_map/pallas_call | solution.py:582
  60.3 1.9 %shard_map.141 = (bf16[128,2048]{1,0:T(8,128)(2,1)}, bf16[2,4,2048]{2,1,0:T(4,128)(2,1)}) custom-call(bf16[128,2048]{1,0:T(8,128)(2,1)} %get-tuple-element.4.a, bf16[2,4,2048]{2,1,0:T(4,128)(2,1)} %get-tuple-element.5.b), custom_call_target="tpu_custom_call" | custom-call | tf_op jit(solution)/shard_map/pallas_call | solution.py:637
